TPU v7x, 256 devices: a whole 4x4x8 slice. The times are simulated.
256 devices in a mesh: ctx: 32 (over y, x, core), head: 8 (over z).
Axes of the slice: x: 4, y: 4, z: 8, core: 2. Of those that a mesh axis runs over, the one named last changes fastest.
Arguments:
- queries: bfloat16 [8192, 4096], P(('ctx', 'head')), may hold values from -0.59765625 to 0.59765625
- key_in: bfloat16 [8192, 4096], P(('ctx', 'head')), may hold values from -0.59765625 to 0.59765625
- values_in: bfloat16 [8192, 4096], P(('ctx', 'head')), may hold values from -6 to 6
- strength: bfloat16 [8192, 32], P(('ctx', 'head')), may hold values from 0 to 0.95, as said below
- log_decay: bfloat16 [8192, 4096], P(('ctx', 'head')), may hold values from -1.2 to 0, as said below
- d_out: bfloat16 [8192, 4096], P(('ctx', 'head')), may hold values from -6 to 6
Outputs:
- d_queries: bfloat16 [8192, 4096], P(('ctx', 'head'))
- d_keys: bfloat16 [8192, 4096], P(('ctx', 'head'))
- d_values: bfloat16 [8192, 4096], P(('ctx', 'head'))
- d_strength: bfloat16 [8192, 32], P(('ctx', 'head'))
- d_log_decay: bfloat16 [8192, 4096], P(('ctx', 'head'))
Inputs may be any that keep to these rules, and one draw needn't show every extreme that they name: `log_decay`: every log decay is negative. Every write strength is positive and below one.
All inputs are finite; a program needn't handle non-finite values.
Results may differ from a plain program's by a relative error of at most 0.00215.
Values may be sent and summed in bfloat16 or wider, within the bound.
No kernel may reach another device: no remote copies, remote signals or barrier semaphores. Data moves between devices by JAX's collectives and lax.ppermute only.
A program may use at most 128 MiB of HBM per device.

v0:
```python
import jax
import jax.numpy as jnp
from jax import lax
from jax.sharding import PartitionSpec as P

SPAN = 64


exact_prec = lax.Precision.HIGHEST
epsilon = 1e-06


def passed_along(value, axis, steps):
    count = lax.axis_size(axis)
    leading, last = (max(0, -steps), min(count, count - steps))
    return lax.ppermute(value, axis, [(source, source + steps) for source in range(leading, last)])


def prepare(queries, keys_used, values_used, strength, log_decay):
    span_len = queries.shape[1]
    head_width = queries.shape[3]
    q_unit = (
        queries
        * lax.rsqrt(jnp.sum(queries * queries, axis=3, keepdims=True) + epsilon)
        * head_width ** (-0.5)
    )
    k_unit = keys_used * lax.rsqrt(jnp.sum(keys_used * keys_used, axis=3, keepdims=True) + epsilon)
    gamma = jnp.cumsum(log_decay, axis=1)
    middle = gamma[:, span_len // 2 - 1 : span_len // 2]
    q_rise = q_unit * jnp.exp(gamma - middle)
    k_rise = k_unit * jnp.exp(gamma - middle)
    k_fall = k_unit * jnp.exp(middle - gamma)
    strict_mask = jnp.tril(jnp.ones((span_len, span_len), jnp.float32), -1)
    causal_mask = jnp.tril(jnp.ones((span_len, span_len), jnp.float32))
    key_inner = jnp.einsum("ntha,nsha->nhts", k_rise, k_fall, precision=exact_prec) * strict_mask
    scores = jnp.einsum("ntha,nsha->nhts", q_rise, k_fall, precision=exact_prec) * causal_mask
    strength_t = jnp.transpose(strength, (0, 2, 1))
    system = jnp.eye(span_len, dtype=jnp.float32) + strength_t[..., None] * key_inner
    k_head = k_unit * jnp.exp(gamma)
    right_side = jnp.concatenate([values_used, k_head], axis=3) * strength[..., None]
    right_side = jnp.transpose(right_side, (0, 2, 1, 3))
    solved = lax.linalg.triangular_solve(
        system, right_side, left_side=True, lower=True, unit_diagonal=True
    )
    w_value = solved[..., :head_width]
    w_key = solved[..., head_width:]
    gamma_end = gamma[:, -1:]
    key_tail = k_unit * jnp.exp(gamma_end - gamma)
    fade_last = jnp.exp(gamma_end[:, 0])
    q_head = q_unit * jnp.exp(gamma)
    return (q_head, scores, w_value, w_key, key_tail, fade_last)


def march(w_value, w_key, key_tail, fade_last, state):

    def advance(state_now, piece_data):
        value_part, key_part, tail_part, fade_part = piece_data
        updates = value_part - jnp.einsum("hta,hab->htb", key_part, state_now, precision=exact_prec)
        following = fade_part[:, :, None] * state_now + jnp.einsum(
            "tha,htb->hab", tail_part, updates, precision=exact_prec
        )
        return (following, (state_now, updates))

    final_state, (start_states, all_updates) = lax.scan(
        advance, state, (w_value, w_key, key_tail, fade_last)
    )
    return (final_state, start_states, all_updates)


def sweep(prepared, state):
    q_head, scores, w_value, w_key, key_tail, fade_last = prepared
    final_state, start_states, all_updates = march(w_value, w_key, key_tail, fade_last, state)
    output = jnp.einsum("ntha,nhab->nthb", q_head, start_states, precision=exact_prec)
    output = output + jnp.einsum("nhts,nhsb->nthb", scores, all_updates, precision=exact_prec)
    return (output, final_state)


def compose(matrix, state):
    return jnp.einsum("hab,hbc->hac", matrix, state, precision=exact_prec)


def per_device(queries, key_in, values_in, strength, log_decay, d_out):
    heads_all = strength.shape[1]
    local_heads = heads_all // lax.axis_size("head")
    head_width = queries.shape[1] // heads_all
    moved = (
        lax.all_to_all(queries, "head", split_axis=1, concat_axis=0, tiled=True),
        lax.all_to_all(key_in, "head", split_axis=1, concat_axis=0, tiled=True),
        lax.all_to_all(values_in, "head", split_axis=1, concat_axis=0, tiled=True),
        lax.all_to_all(log_decay, "head", split_axis=1, concat_axis=0, tiled=True),
        lax.all_to_all(d_out, "head", split_axis=1, concat_axis=0, tiled=True),
        lax.all_to_all(strength, "head", split_axis=1, concat_axis=0, tiled=True),
    )
    query_local, key_local, value_local, decay_local, grad_local, strength_local = moved
    row_count = query_local.shape[0]
    blocks = row_count // SPAN

    def shaped(array):
        return array.astype(jnp.float32).reshape(blocks, SPAN, local_heads, head_width)

    strength_blocks = strength_local.astype(jnp.float32).reshape(blocks, SPAN, local_heads)
    prepared, pull_prep = jax.vjp(
        prepare,
        shaped(query_local),
        shaped(key_local),
        shaped(value_local),
        strength_blocks,
        shaped(decay_local),
    )
    q_head, scores, w_value, w_key, key_tail, fade_last = prepared
    unit_matrix = jnp.broadcast_to(
        jnp.eye(head_width, dtype=jnp.float32), (local_heads, head_width, head_width)
    )
    zero_state = jnp.zeros((local_heads, head_width, head_width), jnp.float32)
    wide_start = jnp.concatenate([zero_state, unit_matrix], axis=2)
    wide_value = jnp.concatenate([w_value, jnp.zeros_like(w_value)], axis=3)
    ends = march(wide_value, w_key, key_tail, fade_last, wide_start)[0]
    offset = ends[..., :head_width]
    transfer = ends[..., head_width:]
    transfer_t = jnp.transpose(transfer, (0, 2, 1))
    cot_out = shaped(grad_local)

    def outputs_of(state):
        return sweep(prepared, state)[0]

    _, pull_state = jax.vjp(outputs_of, zero_state)
    inject = pull_state(cot_out)[0]
    n_context = lax.axis_size("ctx")

    def forward_turn(turn_index, relay_pair):
        leaving, arriving = relay_pair
        arriving = passed_along(leaving, "ctx", 1)
        return (compose(transfer, arriving) + offset, arriving)

    state_in = lax.fori_loop(0, n_context, forward_turn, (offset, zero_state))[1]

    def backward_turn(turn_index, relay_pair):
        leaving, arriving = relay_pair
        arriving = passed_along(leaving, "ctx", -1)
        return (compose(transfer_t, arriving) + inject, arriving)

    grad_in = lax.fori_loop(0, n_context, backward_turn, (inject, zero_state))[1]

    def sweep_prepared(prepared_in):
        return sweep(prepared_in, state_in)

    _, pull_sweep = jax.vjp(sweep_prepared, prepared)
    d_prepared = pull_sweep((cot_out, grad_in))[0]
    d_query, d_key, d_value, d_strength, d_decay = pull_prep(d_prepared)

    def flatten(array):
        return array.reshape(row_count, local_heads * head_width).astype(jnp.bfloat16)

    strength_grad = d_strength.reshape(row_count, local_heads).astype(jnp.bfloat16)
    returned = (
        lax.all_to_all(flatten(d_query), "head", split_axis=0, concat_axis=1, tiled=True),
        lax.all_to_all(flatten(d_key), "head", split_axis=0, concat_axis=1, tiled=True),
        lax.all_to_all(flatten(d_value), "head", split_axis=0, concat_axis=1, tiled=True),
        lax.all_to_all(flatten(d_decay), "head", split_axis=0, concat_axis=1, tiled=True),
        lax.all_to_all(strength_grad, "head", split_axis=0, concat_axis=1, tiled=True),
    )
    return (returned[0], returned[1], returned[2], returned[4], returned[3])


def solution(mesh):
    in_specs = (
        P(("ctx", "head"), None),
        P(("ctx", "head"), None),
        P(("ctx", "head"), None),
        P(("ctx", "head"), None),
        P(("ctx", "head"), None),
        P(("ctx", "head"), None),
    )
    out_specs = (
        P(("ctx", "head"), None),
        P(("ctx", "head"), None),
        P(("ctx", "head"), None),
        P(("ctx", "head"), None),
        P(("ctx", "head"), None),
    )
    return jax.shard_map(
        per_device, mesh=mesh, in_specs=in_specs, out_specs=out_specs, check_vma=False
    )
```

profile of v0, /device:TPU:16, one launch (start us, length us, event | category | flops | bytes accessed | tf_op | source)
XLA Modules:
  0.0 1052.4 jit_solution(14875787865100898344)
XLA Ops:
  2.0 8.5 all-to-all-start.2
  36.2 10.0 all-to-all-done.1
  52.5 79.4 %custom-call.7 = f32[4,4,1,64,64]{3,4,2,1,0:T(8,128)S(1)} custom-call(f32[4,4,1,64,64]{4,3,2,1,0:T(8,128)} %add_bitcast_fusion), custom_call_target="InvertDiagBlocksLowerTriangular" | custom-call | tf_op jit(solution)/shard_map/jvp()/triangular_solve | solution.py:42
  148.0 8.7 while.97
  180.8 11.8 %while.103 = (s32[]{:T(128)}, f32[4,128,128]{2,1,0:T(8,128)S(1)}, f32[4,4,128,128]{3,2,1,0:T(8,128)}, f32[4,4,128,1]{2,1,3,0:T(4,128)S(1)}, f32[4,4,64,128]{3,2,...) while((s32[]{:T(128)}, f32[4,128,128]{2,1,0:T(8,128)S(1)}, ...), condition=%wide.region_13.14_spmd.clone, body=%wide.region_12.13_spmd.clone.sunk | while | flops 101056512 | bytes 1713278 | solution.py:64
  196.4 363.1 %while.98 = (s32[]{:T(128)}, f32[4,128,128]{2,1,0:T(8,128)S(1)}, f32[4,128,128]{2,1,0:T(8,128)}, f32[4,128,128]{2,1,0:T(8,128)}, f32[4,128,128]{2,1,0:T(8,128)}, /*index=5*/s32[]{:T(128)}) while((s32[]{:T(128)}, f32[4,128,128]{2,1,0:T(8,128)S(1)}, f32[4,128,128]{2,1,0:T(8,128)}, f32[4,128,128]{2,1,0:T(8,128)}, f32[4,128,128]{2,1,0:T(8,128)}, ...), condition=%wide.region_5.6_spmd, body=%wide.region_4.5_spmd.sunk | while | flops 100728832 | bytes 3145865 | solution.py:135
  198.3 7.9 collective-permute-done
  209.7 7.9 collective-permute-done
  221.0 7.9 collective-permute-done
  232.4 7.9 collective-permute-done
  243.7 7.9 collective-permute-done
  255.1 7.9 collective-permute-done
  266.4 7.9 collective-permute-done
  277.8 7.9 collective-permute-done
  289.1 7.9 collective-permute-done
  300.5 7.9 collective-permute-done
  311.8 7.9 collective-permute-done
  323.2 7.9 collective-permute-done
  334.5 7.9 collective-permute-done
  345.9 7.9 collective-permute-done
  357.2 7.9 collective-permute-done
  368.5 7.9 collective-permute-done
  391.2 7.9 collective-permute-done
  448.0 7.9 collective-permute-done
  470.7 7.9 collective-permute-done
  527.4 7.9 collective-permute-done
  560.5 15.6 %while.99 = (s32[]{:T(128)}, f32[4,128,128]{2,1,0:T(8,128)S(1)}, f32[4,4,128,128]{3,2,1,0:T(8,128)}, f32[4,4,64,128]{3,2,1,0:T(8,128)}, f32[4,4,128,1]{2,1,3,0:T...) while((s32[]{:T(128)}, f32[4,128,128]{2,1,0:T(8,128)S(1)}, ...), condition=%wide.region_7.8_spmd, body=%wide.region_6.7_spmd.sunk | while | flops 100827136 | bytes 2109549 | solution.py:64
  577.1 351.3 %while.101 = (s32[]{:T(128)}, f32[4,128,128]{2,1,0:T(8,128)}, f32[4,128,128]{2,1,0:T(8,128)}, f32[4,128,128]{2,1,0:T(8,128)S(1)}, f32[4,128,128]{2,1,0:T(8,128)S(1)}, /*index=5*/s32[]{:T(128)}) while((s32[]{:T(128)}, f32[4,128,128]{2,1,0:T(8,128)}, f32[4,128,128]{2,1,0:T(8,128)}, f32[4,128,128]{2,1,0:T(8,128)S(1)}, ...), condition=%wide.region_15.16_spmd, body=%wide.region_14.15_spmd.sunk | while | flops 100728832 | bytes 3145865 | solution.py:142
  931.2 35.2 %while.102 = (s32[]{:T(128)}, f32[4,128,128]{2,1,0:T(8,128)S(1)}, f32[4,4,64,128]{3,2,1,0:T(8,128)}, f32[4,4,64,128]{3,2,1,0:T(8,128)}, f32[4,64,4,128]{3,1,2,0:...) while((s32[]{:T(128)}, f32[4,128,128]{2,1,0:T(8,128)S(1)}, ...), condition=%wide.region_18.19_spmd, body=%wide.region_16.18_spmd.sunk | while | flops 201752064 | bytes 3424421 | solution.py:64
  1001.4 8.4 all-to-all-done.7
  1014.7 9.2 all-to-all-done.10
  1028.4 9.5 all-to-all-done.6
  (564 shorter events, 766.8 us)
Async XLA Ops:
  2.0 16.2 %all-to-all-start.2 = ((bf16[32,8,4]{0,2,1:T(4,128)(2,1)}), bf16[32,8,4]{0,2,1:T(4,128)(2,1)S(1)}, u32[]{:S(2)}, u32[]{:S(2)}) async-start(bf16[32,8,4]{0,2,1:T(4,128)(2,1)} %bitcast.27), calls=%async_computation.2 | async-start | bytes 16384 | tf_op jit(solution)/shard_map/all_to_all | solution.py:92
  18.2 14.2 %all-to-all-start = ((bf16[32,8,512]{2,0,1:T(8,128)(2,1)}), bf16[32,8,512]{2,0,1:T(8,128)(2,1)S(1)}, u32[]{:S(2)}, u32[]{:S(2)}) async-start(bf16[32,8,512]{2,0,1:T(8,128)(2,1)} %bitcast.215), calls=%async_computation | async-start | bytes 524288 | tf_op jit(solution)/shard_map/all_to_all | solution.py:90
  32.4 13.8 %all-to-all-start.1 = ((bf16[32,8,512]{2,0,1:T(8,128)(2,1)}), bf16[32,8,512]{2,0,1:T(8,128)(2,1)S(1)}, u32[]{:S(2)}, u32[]{:S(2)}) async-start(bf16[32,8,512]{2,0,1:T(8,128)(2,1)} %bitcast.214), calls=%async_computation.1 | async-start | bytes 524288 | tf_op jit(solution)/shard_map/all_to_all | solution.py:88
  46.2 86.7 %all-to-all-start.3 = ((bf16[32,8,512]{2,0,1:T(8,128)(2,1)}), bf16[32,8,512]{2,0,1:T(8,128)(2,1)S(1)}, u32[]{:S(2)}, u32[]{:S(2)}) async-start(bf16[32,8,512]{2,0,1:T(8,128)(2,1)} %bitcast.213), calls=%async_computation.3 | async-start | bytes 524288 | tf_op jit(solution)/shard_map/all_to_all | solution.py:89
  133.7 23.0 %all-to-all-start.5 = ((bf16[32,8,512]{2,0,1:T(8,128)(2,1)}), bf16[32,8,512]{2,0,1:T(8,128)(2,1)}, u32[]{:S(2)}, u32[]{:S(2)}) async-start(bf16[32,8,512]{2,0,1:T(8,128)(2,1)} %bitcast.211), calls=%async_computation.5 | async-start | bytes 524288 | tf_op jit(solution)/shard_map/all_to_all | solution.py:87
  156.7 17.7 %all-to-all-start.4 = ((bf16[32,8,512]{2,0,1:T(8,128)(2,1)}), bf16[32,8,512]{2,0,1:T(8,128)(2,1)S(1)}, u32[]{:S(2)}, u32[]{:S(2)}) async-start(bf16[32,8,512]{2,0,1:T(8,128)(2,1)} %bitcast.212), calls=%async_computation.4 | async-start | bytes 524288 | tf_op jit(solution)/shard_map/all_to_all | solution.py:91
  584.3 10.0 collective-permute-start.1
  606.5 10.0 collective-permute-start.1
  628.7 10.0 collective-permute-start.1
  639.8 10.0 collective-permute-start.1
  650.9 10.0 collective-permute-start.1
  662.0 10.0 collective-permute-start.1
  684.2 10.0 collective-permute-start.1
  706.4 10.0 collective-permute-start.1
  717.5 10.0 collective-permute-start.1
  739.7 10.0 collective-permute-start.1
  750.8 10.0 collective-permute-start.1
  761.9 10.0 collective-permute-start.1
  773.1 10.0 collective-permute-start.1
  795.3 10.0 collective-permute-start.1
  817.5 10.0 collective-permute-start.1
  828.6 10.0 collective-permute-start.1
  839.7 10.0 collective-permute-start.1
  850.8 10.0 collective-permute-start.1
  861.9 10.0 collective-permute-start.1
  873.0 10.0 collective-permute-start.1
  884.1 10.0 collective-permute-start.1
  979.8 12.4 %all-to-all-start.9 = ((bf16[8,32,4]{1,2,0:T(4,128)(2,1)}), bf16[8,32,4]{1,2,0:T(4,128)(2,1)}, u32[]{:S(2)}, u32[]{:S(2)}) async-start(bf16[8,32,4]{1,2,0:T(4,128)(2,1)} %copy.315), calls=%async_computation.9 | async-start | bytes 16384 | tf_op jit(solution)/shard_map/all_to_all | solution.py:160
  992.2 17.7 %all-to-all-start.7 = ((bf16[8,32,512]{2,1,0:T(8,128)(2,1)}), bf16[8,32,512]{2,1,0:T(8,128)(2,1)S(1)}, u32[]{:S(2)}, u32[]{:S(2)}) async-start(bf16[8,32,512]{2,1,0:T(8,128)(2,1)} %convert_element_type.118), calls=%async_computation.7 | async-start | bytes 524288 | tf_op jit(solution)/shard_map/all_to_all | solution.py:157
  1009.9 14.0 %all-to-all-start.10 = ((bf16[8,32,512]{2,1,0:T(8,128)(2,1)}), bf16[8,32,512]{2,1,0:T(8,128)(2,1)S(1)}, u32[]{:S(2)}, u32[]{:S(2)}) async-start(bf16[8,32,512]{2,1,0:T(8,128)(2,1)} %convert_element_type.123), calls=%async_computation.10 | async-start | bytes 524288 | tf_op jit(solution)/shard_map/all_to_all | solution.py:159
  1023.9 14.0 %all-to-all-start.6 = ((bf16[8,32,512]{2,1,0:T(8,128)(2,1)}), bf16[8,32,512]{2,1,0:T(8,128)(2,1)S(1)}, u32[]{:S(2)}, u32[]{:S(2)}) async-start(bf16[8,32,512]{2,1,0:T(8,128)(2,1)} %convert_element_type.116), calls=%async_computation.6 | async-start | bytes 524288 | tf_op jit(solution)/shard_map/all_to_all | solution.py:156
  1037.9 13.8 %all-to-all-start.8 = ((bf16[8,32,512]{2,1,0:T(8,128)(2,1)}), bf16[8,32,512]{2,1,0:T(8,128)(2,1)S(1)}, u32[]{:S(2)}, u32[]{:S(2)}) async-start(bf16[8,32,512]{2,1,0:T(8,128)(2,1)} %convert_element_type.119), calls=%async_computation.8 | async-start | bytes 524288 | tf_op jit(solution)/shard_map/all_to_all | solution.py:158
  (142 other events, 619.5 us)
where the time goes:
time: 1060 us; the launch traced here: 1050 us
  waiting for transfers between devices  446 us (42%)
  starting transfers between devices  298 us (28%)
  matrix products  167 us (16%)
  other arithmetic  93.7 us (9%)
  local copies, waits for them, and re-layouts  44.8 us (4%)
    ppermute x64, waiting for transfers between devices, passed_along(): lax.ppermute(value, axis, [(source, source + steps) for source in range(l...  386 us
    ppermute x64, starting transfers between devices, passed_along(): lax.ppermute(value, axis, [(source, source + steps) for source in range(l...  243 us
    dot_general x64, matrix products, compose(): return jnp.einsum('hab,hbc->hac', matrix, state, precision=exact_prec)  83.5 us
    another operation x5, other arithmetic, prepare(): lax.linalg.triangular_solve(system, right_side, left_side=True, lower=Tru...  80.4 us
    dot_general x20, matrix products, advance(): jnp.einsum('hta,hab->htb', key_part, state_now, precision=exact_prec)  35 us
    dot_general x20, matrix products, advance(): jnp.einsum('tha,htb->hab', tail_part, updates, precision=exact_prec)  23.4 us
  transfers between devices with their start and end apart: 75, of which 72 were waited for; matrix products, arithmetic and copies ran while one was open for 12% of the time, Pallas kernels for 0%

commit v1 on v0

v1 whole, which is shorter than its diff:
```python
import jax
import jax.numpy as jnp
from jax import lax
from jax.experimental import pallas as pl
from jax.experimental.pallas import tpu as pltpu
from jax.sharding import Mesh, PartitionSpec as P

epsilon = 1e-06
bf16 = jnp.bfloat16
f32 = jnp.float32
CHUNK = 128
VMEM_BYTES = 56 << 20


def params():
    return pltpu.CompilerParams(vmem_limit_bytes=VMEM_BYTES)


def parts(value):
    high = value.astype(bf16)
    return (high, (value - high.astype(f32)).astype(bf16))


def beside(arrays, axis):
    return arrays[0] if len(arrays) == 1 else jnp.concatenate(arrays, axis)


def product(left, right, left_axis=1, right_axis=0):
    wide = right[0].shape[1 - right_axis]
    row = beside(right, 1 - right_axis)
    stacked = beside([row] * len(left), right_axis)
    lengthened = beside(left, left_axis)
    found = lax.dot_general(
        lengthened, stacked, (((left_axis,), (right_axis,)), ((), ())), preferred_element_type=f32
    )
    if len(right) == 1:
        return found
    return found[:, :wide] + found[:, wide:]


def indices():
    rows = lax.broadcasted_iota(jnp.int32, (CHUNK, CHUNK), 0)
    columns = lax.broadcasted_iota(jnp.int32, (CHUNK, CHUNK), 1)
    return rows, columns


def strength_of(packed):
    sources, half, lanes = packed.shape
    packed = packed.astype(f32)
    first = jnp.broadcast_to(packed[:, :, 0:1], (sources, half, lanes))
    second = jnp.broadcast_to(packed[:, :, lanes // 2 : lanes // 2 + 1], (sources, half, lanes))
    return jnp.concatenate([first, second], axis=1).reshape(sources * 2 * half, lanes)


def rows_of(ref, piece, start, count):
    sources = CHUNK // 32
    block = ref[piece * sources : (piece + 1) * sources, start : start + count, :]
    return block


def chunk_of(ref, piece, start):
    return rows_of(ref, piece, start, 32).reshape(CHUNK, ref.shape[2])


def key_terms(first_ref, piece, causal_ones):
    key = chunk_of(first_ref, piece, 0).astype(f32)
    decay = chunk_of(first_ref, piece, 32)
    weight = strength_of(rows_of(first_ref, piece, 64, 16))
    gamma = jnp.dot(causal_ones, decay, preferred_element_type=f32)
    middle = gamma[CHUNK // 2 - 1 : CHUNK // 2]
    last = gamma[CHUNK - 1 : CHUNK]
    inverse = lax.rsqrt(jnp.sum(key * key, axis=1, keepdims=True) + epsilon)
    unit = key * inverse
    rise = jnp.exp(gamma - middle)
    fall = jnp.exp(middle - gamma)
    head = jnp.exp(gamma)
    tail = jnp.exp(last - gamma)
    return dict(
        unit=unit, inverse=inverse, weight=weight, rise=rise, fall=fall, head=head, tail=tail, fade=jnp.exp(last)
    )


def spread_kernel(heads, first, second, third, *rest):
    *strength, out_ref = rest
    span = first.shape[0]
    for head in range(heads):
        lanes = slice(head * 128, (head + 1) * 128)
        out_ref[head, 0:span, :] = first[:, lanes]
        out_ref[head, span : 2 * span, :] = second[:, lanes]
        if third is not None:
            out_ref[head, 2 * span : 3 * span, :] = third[:, lanes]
    if strength:
        values = strength[0][...].astype(f32)
        half = span // 2
        early = lax.broadcasted_iota(jnp.int32, (half, 128), 1) < 64
        for head in range(heads):
            column = values[:, head : head + 1]
            packed = jnp.where(early, column[:half], column[half:])
            out_ref[head, 2 * span : 2 * span + half, :] = packed.astype(bf16)


def spread_keys(key_in, log_decay, strength):
    heads = strength.shape[1]

    def body(key_ref, decay_ref, strength_ref, out_ref):
        spread_kernel(heads, key_ref, decay_ref, None, strength_ref, out_ref)

    return pl.pallas_call(
        body, out_shape=jax.ShapeDtypeStruct((heads, 80, 128), bf16), compiler_params=params(), name="spread_keys"
    )(key_in, log_decay, strength)


def spread_values(values_in, queries, d_out, heads):
    def body(value_ref, query_ref, grad_ref, out_ref):
        spread_kernel(heads, value_ref, query_ref, grad_ref, out_ref)

    return pl.pallas_call(
        body, out_shape=jax.ShapeDtypeStruct((heads, 96, 128), bf16), compiler_params=params(), name="spread_values"
    )(values_in, queries, d_out)


def tree_levels(count):
    nodes = list(range(count))
    following = count
    found = []
    while len(nodes) > 1:
        above = []
        for left, right in zip(nodes[0::2], nodes[1::2]):
            found.append((following, left, right))
            above.append(following)
            following += 1
        nodes = above
    return found


def keys_kernel(pieces, first_ref, solve_ref, inner_ref, wkey_ref, transfer_ref):
    rows, columns = indices()
    causal_ones = jnp.where(rows >= columns, 1.0, 0.0).astype(bf16)
    strict = rows > columns
    eye = jnp.where(rows == columns, 1.0, 0.0)
    terms = [key_terms(first_ref, piece, causal_ones) for piece in range(pieces)]
    systems = []
    solved = []
    for piece in range(pieces):
        t = terms[piece]
        inner = product(parts(t["unit"] * t["rise"]), parts(t["unit"] * t["fall"]), 1, 1)
        inner = jnp.where(strict, inner, 0.0)
        inner_ref[piece] = inner
        system = t["weight"] * inner
        systems.append(system)
        pair = ((rows ^ columns) == 1) & strict
        solved.append(eye - jnp.where(pair, system, 0.0))
    shift = 1
    while (1 << shift) < CHUNK:
        row_block = lax.shift_right_logical(rows, shift)
        column_block = lax.shift_right_logical(columns, shift)
        corner = (row_block == column_block + 1) & ((row_block & 1) == 1)
        for piece in range(pieces):
            inverse = parts(solved[piece])
            block = parts(jnp.where(corner, systems[piece], 0.0))
            between = product(parts(product(inverse, block)), inverse)
            solved[piece] = solved[piece] - between
        shift += 1
    for piece in range(pieces):
        t = terms[piece]
        solve_ref[piece] = solved[piece]
        weighted = parts(t["weight"] * (t["unit"] * t["head"]))
        wkey = product(parts(solved[piece]), weighted)
        wkey_ref[piece] = wkey
        tail = parts(t["unit"] * t["tail"])
        transfer_ref[piece] = eye * t["fade"] - product(tail, parts(wkey), 0, 0)
    for parent, left, right in tree_levels(pieces):
        transfer_ref[parent] = product(parts(transfer_ref[right]), parts(transfer_ref[left]))


def keys_stage(first):
    pieces = first.shape[0] * 32 // CHUNK
    square = jax.ShapeDtypeStruct((pieces, CHUNK, CHUNK), f32)
    tree = jax.ShapeDtypeStruct((2 * pieces - 1, CHUNK, CHUNK), f32)

    def body(*refs):
        keys_kernel(pieces, *refs)

    return pl.pallas_call(
        body, out_shape=(square, square, square, tree), compiler_params=params(), name="keys_stage"
    )(first)


def query_terms(second_ref, piece):
    query = chunk_of(second_ref, piece, 32).astype(f32)
    inverse = lax.rsqrt(jnp.sum(query * query, axis=1, keepdims=True) + epsilon)
    return query * inverse, inverse


def values_kernel(
    pieces, first_ref, second_ref, solve_ref, wkey_ref, transfer_ref, wvalue_ref, scores_ref, offset_ref, inject_ref
):
    rows, columns = indices()
    causal_ones = jnp.where(rows >= columns, 1.0, 0.0).astype(bf16)
    causal = rows >= columns
    scale = CHUNK ** (-0.5)
    for piece in range(pieces):
        t = key_terms(first_ref, piece, causal_ones)
        query = query_terms(second_ref, piece)[0] * scale
        scores = product(parts(query * t["rise"]), parts(t["unit"] * t["fall"]), 1, 1)
        scores = jnp.where(causal, scores, 0.0)
        scores_ref[piece] = scores
        value = chunk_of(second_ref, piece, 0).astype(f32)
        wvalue = product(parts(solve_ref[piece]), parts(t["weight"] * value))
        wvalue_ref[piece] = wvalue
        offset_ref[piece] = product(parts(t["unit"] * t["tail"]), parts(wvalue), 0, 0)
        reach = query * t["head"] - product(parts(scores), parts(wkey_ref[piece]))
        grad = chunk_of(second_ref, piece, 64)
        inject_ref[piece] = product(parts(reach), (grad,), 0, 0)
    for parent, left, right in tree_levels(pieces):
        offset_ref[parent] = (
            product(parts(transfer_ref[right]), parts(offset_ref[left])) + offset_ref[right]
        )
        inject_ref[parent] = inject_ref[left] + product(
            parts(transfer_ref[left]), parts(inject_ref[right]), 0, 0
        )


def values_stage(first, second, solve, wkey, transfer):
    pieces = first.shape[0] * 32 // CHUNK
    square = jax.ShapeDtypeStruct((pieces, CHUNK, CHUNK), f32)
    tree = jax.ShapeDtypeStruct((2 * pieces - 1, CHUNK, CHUNK), f32)

    def body(*refs):
        values_kernel(pieces, *refs)

    return pl.pallas_call(
        body, out_shape=(square, square, tree, tree), compiler_params=params(), name="values_stage"
    )(first, second, solve, wkey, transfer)


def grads_kernel(
    pieces,
    blocks,
    place_ref,
    first_ref,
    second_ref,
    solve_ref,
    inner_ref,
    wkey_ref,
    transfer_ref,
    wvalue_ref,
    scores_ref,
    offset_ref,
    inject_ref,
    far_transfer_ref,
    far_ref,
    out_ref,
    state_ref,
    cot_ref,
):
    rows, columns = indices()
    causal = rows >= columns
    strict = rows > columns
    causal_ones = jnp.where(causal, 1.0, 0.0).astype(bf16)
    reverse_ones = jnp.where(rows <= columns, 1.0, 0.0).astype(bf16)
    sum_ones = jnp.ones((16, CHUNK), bf16)
    early = lax.broadcasted_iota(jnp.int32, (CHUNK // 32, 16, CHUNK), 2) < CHUNK // 2
    scale = CHUNK ** (-0.5)
    place = place_ref[0]
    state = jnp.where(place > 0, far_ref[0], 0.0)
    cot = jnp.where(place < blocks - 1, far_ref[blocks - 1], 0.0)
    for step in range(1, blocks - 1):
        back = blocks - 1 - step
        moved = product(parts(far_transfer_ref[step]), parts(state)) + far_ref[step]
        returned = product(parts(far_transfer_ref[back]), parts(cot), 0, 0) + far_ref[back]
        state = jnp.where(place > step, moved, state)
        cot = jnp.where(place < back, returned, cot)
    state_ref[2 * pieces - 2] = state
    cot_ref[2 * pieces - 2] = cot
    for parent, left, right in reversed(tree_levels(pieces)):
        state = state_ref[parent]
        cot = cot_ref[parent]
        state_ref[left] = state
        state_ref[right] = product(parts(transfer_ref[left]), parts(state)) + offset_ref[left]
        cot_ref[right] = cot
        cot_ref[left] = product(parts(transfer_ref[right]), parts(cot), 0, 0) + inject_ref[right]
    for piece in range(pieces):
        t = key_terms(first_ref, piece, causal_ones)
        query_one, query_inverse = query_terms(second_ref, piece)
        query = query_one * scale
        value = chunk_of(second_ref, piece, 0).astype(f32)
        grad = chunk_of(second_ref, piece, 64)
        state = state_ref[piece]
        cot = cot_ref[piece]
        state_parts = parts(state)
        cot_parts = parts(cot)
        unit = t["unit"]
        key_rise = unit * t["rise"]
        key_fall = unit * t["fall"]
        key_head = unit * t["head"]
        key_tail = unit * t["tail"]
        update = wvalue_ref[piece] - product(parts(wkey_ref[piece]), state_parts)
        update_parts = parts(update)
        d_update = product(parts(scores_ref[piece]), (grad,), 0, 0) + product(parts(key_tail), cot_parts)
        d_right = product(parts(solve_ref[piece]), parts(d_update), 0, 0)
        d_value = t["weight"] * d_right
        missed = value - product(parts(key_head), state_parts)
        missed = missed - product(parts(inner_ref[piece]), update_parts)
        d_weight = jnp.sum(d_right * missed, axis=1, keepdims=True)
        d_value_parts = parts(d_value)
        wide = CHUNK
        d_query_head = product((grad,), state_parts, 1, 1)
        d_key_head = -product(d_value_parts, state_parts, 1, 1)
        d_key_tail = product(update_parts, cot_parts, 1, 1)
        d_scores = jnp.where(causal, product((grad,), update_parts, 1, 1), 0.0)
        d_inner = jnp.where(strict, -product(d_value_parts, update_parts, 1, 1), 0.0)
        d_scores_parts = parts(d_scores)
        d_inner_parts = parts(d_inner)
        fall_parts = parts(key_fall)
        query_rise = query * t["rise"]
        d_query_rise = product(d_scores_parts, fall_parts)
        d_key_rise = product(d_inner_parts, fall_parts)
        d_key_fall = product(d_scores_parts, parts(query_rise), 0, 0) + product(
            d_inner_parts, parts(key_rise), 0, 0
        )
        d_query_unit = d_query_rise * t["rise"] + d_query_head * t["head"]
        up = d_key_rise * t["rise"] + d_key_head * t["head"]
        tail_term = d_key_tail * t["tail"]
        down = d_key_fall * t["fall"] + tail_term
        d_key_unit = up + down
        d_gamma = query * d_query_unit + unit * (up - down)
        faded = cot * state
        faded_high, faded_low = parts(faded)
        faded_rest = (faded - faded_high.astype(f32) - faded_low.astype(f32)).astype(bf16)
        d_fade = product((sum_ones,), (faded_high, faded_low), 1, 1) + product(
            (sum_ones,), (faded_rest,), 1, 1
        )
        d_last = jnp.sum(unit * tail_term, axis=0, keepdims=True) + d_fade[0:1] * t["fade"]
        gamma_high, gamma_low = parts(d_gamma)
        gamma_rest = (d_gamma - gamma_high.astype(f32) - gamma_low.astype(f32)).astype(bf16)
        d_decay = (
            product((reverse_ones,), (gamma_high, gamma_low))
            + product((reverse_ones,), (gamma_rest,))
            + d_last
        )
        d_query = (scale * query_inverse) * (
            d_query_unit - query_one * jnp.sum(query_one * d_query_unit, axis=1, keepdims=True)
        )
        d_key = t["inverse"] * (d_key_unit - unit * jnp.sum(unit * d_key_unit, axis=1, keepdims=True))
        sources = CHUNK // 32
        span = slice(piece * sources, (piece + 1) * sources)

        def shaped(array):
            return array.astype(bf16).reshape(sources, 32, wide)

        out_ref[span, 0:32, :] = shaped(d_query)
        out_ref[span, 32:64, :] = shaped(d_key)
        out_ref[span, 64:96, :] = shaped(d_value)
        out_ref[span, 96:128, :] = shaped(d_decay)
        weights = jnp.broadcast_to(d_weight, (CHUNK, CHUNK)).reshape(sources, 32, CHUNK)
        out_ref[span, 128:144, :] = jnp.where(early, weights[:, :16], weights[:, 16:]).astype(bf16)


def grads_stage(place, blocks, *arrays):
    first = arrays[0]
    sources = first.shape[0]
    pieces = sources * 32 // CHUNK

    def body(*refs):
        grads_kernel(pieces, blocks, *refs)

    return pl.pallas_call(
        body,
        in_specs=[pl.BlockSpec(memory_space=pltpu.SMEM)] + [pl.BlockSpec(memory_space=pltpu.VMEM)] * len(arrays),
        out_specs=pl.BlockSpec(memory_space=pltpu.VMEM),
        out_shape=jax.ShapeDtypeStruct((sources, 144, CHUNK), bf16),
        scratch_shapes=[pltpu.VMEM((2 * pieces - 1, CHUNK, CHUNK), f32)] * 2,
        compiler_params=params(),
        name="grads_stage",
    )(place, *arrays)


def unspread_kernel(packed_ref, query_ref, key_ref, value_ref, strength_ref, decay_ref):
    heads = packed_ref.shape[0]
    span = query_ref.shape[0]
    for head in range(heads):
        lanes = slice(head * 128, (head + 1) * 128)
        query_ref[:, lanes] = packed_ref[head, 0:span, :]
        key_ref[:, lanes] = packed_ref[head, span : 2 * span, :]
        value_ref[:, lanes] = packed_ref[head, 2 * span : 3 * span, :]
        decay_ref[:, lanes] = packed_ref[head, 3 * span : 4 * span, :]
    place = lax.broadcasted_iota(jnp.int32, (span, 128), 1)
    total = jnp.zeros((span, 128), f32)
    for head in range(heads):
        column = strength_of(packed_ref[head : head + 1, 4 * span : 4 * span + span // 2, :])
        total = jnp.where(place == head, column, total)
    strength_ref[...] = total[:, :heads].astype(bf16)


def unspread(packed, span):
    heads = packed.shape[0]
    wide = jax.ShapeDtypeStruct((span, heads * 128), bf16)
    return pl.pallas_call(
        unspread_kernel,
        out_shape=(wide, wide, wide, jax.ShapeDtypeStruct((span, heads), bf16), wide),
        compiler_params=params(),
        name="unspread",
    )(packed)


def per_device(queries, key_in, values_in, strength, log_decay, d_out):
    heads = strength.shape[1]
    blocks = lax.axis_size("block")
    place = lax.axis_index("block")

    def swap(array):
        return lax.all_to_all(array, ("near", "head"), 0, 0, tiled=True)

    def share(array):
        return lax.all_to_all(array, "block", 0, 0, tiled=True)

    first = swap(spread_keys(key_in, log_decay, strength))
    second = swap(spread_values(values_in, queries, d_out, heads))
    solve, inner, wkey, transfer = keys_stage(first)
    whole = (blocks, CHUNK, CHUNK)
    far_transfer = share(jnp.broadcast_to(transfer[-1], whole))
    wvalue, scores, offset, inject = values_stage(first, second, solve, wkey, transfer)
    later = lax.broadcasted_iota(jnp.int32, whole, 0) > place
    far = share(jnp.where(later, offset[-1], inject[-1]))
    packed = grads_stage(
        place.astype(jnp.int32).reshape(1),
        blocks,
        first,
        second,
        solve,
        inner,
        wkey,
        transfer,
        wvalue,
        scores,
        offset,
        inject,
        far_transfer,
        far,
    )
    return unspread(swap(packed), queries.shape[0])


def solution(mesh):
    heads_axis = mesh.shape["head"]
    near = 32 // heads_axis
    wide = Mesh(mesh.devices.reshape(-1, near, heads_axis), ("block", "near", "head"))
    spec = P(("block", "near", "head"), None)
    return jax.shard_map(
        per_device, mesh=wide, in_specs=(spec,) * 6, out_specs=(spec,) * 5, check_vma=False
    )
```

time: 1060 us -> 147 us (0.14)
  the two profiles are of different devices: /device:TPU:16 before, /device:TPU:1 now
where the time goes in v1:
time: 147 us; the launch traced here: 146 us
  blocking collectives  52.9 us (36%)
  waiting for transfers between devices  34.3 us (23%)
  Pallas kernels  32.6 us (22%)
  starting transfers between devices  22.8 us (16%)
  local copies, waits for them, and re-layouts  2.6 us (2%)
    all_to_all x1, blocking collectives, swap(): return lax.all_to_all(array, ('near', 'head'), 0, 0, tiled=True)  38.8 us
    all_to_all x2, waiting for transfers between devices, swap(): return lax.all_to_all(array, ('near', 'head'), 0, 0, tiled=True)  31.2 us
    all_to_all x2, starting transfers between devices, swap(): return lax.all_to_all(array, ('near', 'head'), 0, 0, tiled=True)  16.4 us
    all_to_all x1, blocking collectives, share(): return lax.all_to_all(array, 'block', 0, 0, tiled=True)  14.1 us
    pallas_call x1, Pallas kernels, grads_stage(): pl.pallas_call(body, in_specs=[pl.BlockSpec(memory_space=pltpu.SMEM)] + [...  13.5 us
    pallas_call x1, Pallas kernels, values_stage(): pl.pallas_call(body, out_shape=(square, square, tree, tree), compiler_par...  7.06 us
    all_to_all x1, starting transfers between devices, share(): return lax.all_to_all(array, 'block', 0, 0, tiled=True)  6.36 us
    pallas_call x1, Pallas kernels, keys_stage(): pl.pallas_call(body, out_shape=(square, square, square, tree), compiler_p...  5.57 us
  transfers between devices with their start and end apart: 3, of which 3 were waited for; matrix products, arithmetic and copies ran while one was open for 1% of the time, Pallas kernels for 10%

profile of v1, /device:TPU:1, one launch (start us, length us, event | category | flops | bytes accessed | tf_op | source)
XLA Modules:
  0.0 146.0 jit_solution(9981658849687159815)
XLA Ops:
  0.6 2.1 %spread_keys.1 = bf16[32,80,128]{2,1,0:T(8,128)(2,1)} custom-call(bf16[32,4096]{1,0:T(8,128)(2,1)} %key_ref.1, bf16[32,4096]{1,0:T(8,128)(2,1)} %decay_ref.1, bf16[32,32]{1,0:T(8,128)(2,1)} %strength_ref.1), custom_call_target="tpu_custom_call" | custom-call | tf_op jit(solution)/shard_map/spread_keys/pallas_call | solution.py:108
  2.7 11.1 %all-to-all-start = ((bf16[32,80,128]{2,1,0:T(8,128)(2,1)}), bf16[32,80,128]{2,1,0:T(8,128)(2,1)S(1)}, u32[]{:S(2)}, u32[]{:S(2)}) async-start(bf16[32,80,128]{2,1,0:T(8,128)(2,1)} %spread_keys.1), calls=%async_computation | async-start | bytes 1310720 | tf_op jit(solution)/shard_map/all_to_all | solution.py:413
  13.8 2.1 %spread_values.1 = bf16[32,96,128]{2,1,0:T(8,128)(2,1)} custom-call(bf16[32,4096]{1,0:T(8,128)(2,1)} %value_ref.1, bf16[32,4096]{1,0:T(8,128)(2,1)} %query_ref.1, bf16[32,4096]{1,0:T(8,128)(2,1)} %grad_ref.1), custom_call_target="tpu_custom_call" | custom-call | tf_op jit(solution)/shard_map/spread_values/pallas_call | solution.py:117
  15.9 16.5 %all-to-all-done.refs_0_.refs_1_ = bf16[32,80,128]{2,1,0:T(8,128)(2,1)S(1)} async-done(((bf16[32,80,128]{2,1,0:T(8,128)(2,1)}), bf16[32,80,128]{2,1,0:T(8,128)(2,1)S(1)}, u32[]{:S(2)}, u32[]{:S(2)}) %all-to-all-start) | async-done | bytes 655392 | tf_op jit(solution)/shard_map/all_to_all | solution.py:413
  32.4 0.0 copy-start
  32.4 5.3 %all-to-all-start.1 = ((bf16[32,96,128]{2,1,0:T(8,128)(2,1)}), bf16[32,96,128]{2,1,0:T(8,128)(2,1)S(1)}, u32[]{:S(2)}, u32[]{:S(2)}) async-start(bf16[32,96,128]{2,1,0:T(8,128)(2,1)} %spread_values.1), calls=%async_computation.1 | async-start | bytes 1572864 | tf_op jit(solution)/shard_map/all_to_all | solution.py:413
  37.8 0.0 copy-done
  37.8 5.6 %keys_stage.1 = (f32[8,128,128]{2,1,0:T(8,128)}, f32[8,128,128]{2,1,0:T(8,128)}, f32[8,128,128]{2,1,0:T(8,128)}, f32[15,128,128]{2,1,0:T(8,128)}) custom-call(bf16[32,80,128]{2,1,0:T(8,128)(2,1)} %copy-done), custom_call_target="tpu_custom_call" | custom-call | tf_op jit(solution)/shard_map/keys_stage/pallas_call | solution.py:184
  43.4 0.8 slice_bitcast_fusion.2
  44.2 14.7 %all-to-all-done.1.refs_1_.refs_2_ = bf16[32,96,128]{2,1,0:T(8,128)(2,1)S(1)} async-done(((bf16[32,96,128]{2,1,0:T(8,128)(2,1)}), bf16[32,96,128]{2,1,0:T(8,128)(2,1)S(1)}, u32[]{:S(2)}, u32[]{:S(2)}) %all-to-all-start.1) | async-done | bytes 786464 | tf_op jit(solution)/shard_map/all_to_all | solution.py:413
  58.9 0.0 copy-start.1
  58.9 0.9 broadcast_in_dim.11
  59.8 6.4 %all-to-all-start.2 = ((f32[8,128,128]{2,1,0:T(8,128)}), f32[8,128,128]{2,1,0:T(8,128)S(1)}, u32[]{:S(2)}, u32[]{:S(2)}) async-start(f32[8,128,128]{2,1,0:T(8,128)} %broadcast_in_dim.11), calls=%async_computation.2 | async-start | bytes 1048576 | tf_op jit(solution)/shard_map/all_to_all | solution.py:416
  66.1 0.0 copy-done.1
  66.1 7.1 %values_stage.1 = (f32[8,128,128]{2,1,0:T(8,128)}, f32[8,128,128]{2,1,0:T(8,128)}, f32[15,128,128]{2,1,0:T(8,128)}, f32[15,128,128]{2,1,0:T(8,128)}) custom-call(bf16[32,80,128]{2,1,0:T(8,128)(2,1)} %copy-done, bf16[32,96,128]{2,1,0:T(8,128)(2,1)} %copy-done.1, f32[8,128,128]{2,1,0:T(8,128)} %get-tuple-element.13.refs_2_.refs_3_, ...), custom_call_target="tpu_custom_call" | custom-call | tf_op jit(solution)/shard_map/values_stage/pallas_call | solution.py:232
  73.2 0.9 slice_bitcast_fusion
  74.1 0.1 broadcast_select_fusion
  74.2 3.1 %all-to-all-done.2.refs_11_ = f32[8,128,128]{2,1,0:T(8,128)S(1)} async-done(((f32[8,128,128]{2,1,0:T(8,128)}), f32[8,128,128]{2,1,0:T(8,128)S(1)}, u32[]{:S(2)}, u32[]{:S(2)}) %all-to-all-start.2) | async-done | bytes 524320 | tf_op jit(solution)/shard_map/all_to_all | solution.py:416
  77.3 0.0 copy-start.2
  77.3 14.1 %all_to_all.25.refs_12_ = f32[8,128,128]{2,1,0:T(8,128)} all-to-all(f32[8,128,128]{2,1,0:T(8,128)S(1)} %broadcast_select_fusion), channel_id=1, replica_groups=mesh['block'=8,'near'=4,'head'=8] {'block'}, dimensions={0} | all-to-all | bytes 1048576 | tf_op jit(solution)/shard_map/all_to_all | solution.py:416
  91.4 0.0 copy-done.2
  91.4 13.5 %grads_stage.1 = bf16[32,144,128]{2,1,0:T(8,128)(2,1)} custom-call(s32[1]{0:T(128)} %bitcast.refs_0_, bf16[32,80,128]{2,1,0:T(8,128)(2,1)} %copy-done, bf16[32,96,128]{2,1,0:T(8,128)(2,1)} %copy-done.1, f32[8,128,128]{2,1,0:T(8,128)} %get-tuple-element.13.refs_2_.refs_3_, f32[8,128,128]{2,1,0:T(8,128)} %get-tuple-element.14.refs_4_, ...), custom_call_target="tpu_custom_call" | custom-call | tf_op jit(solution)/shard_map/grads_stage/pallas_call | solution.py:368
  104.8 38.8 %all_to_all.26.packed_ref = bf16[32,144,128]{2,1,0:T(8,128)(2,1)} all-to-all(bf16[32,144,128]{2,1,0:T(8,128)(2,1)} %grads_stage.1), channel_id=1, replica_groups=mesh['block'=8,'near'=4,'head'=8] {'near','head'}, dimensions={0} | all-to-all | bytes 2359296 | tf_op jit(solution)/shard_map/all_to_all | solution.py:413
  143.6 2.3 %unspread.1 = (bf16[32,4096]{1,0:T(8,128)(2,1)}, bf16[32,4096]{1,0:T(8,128)(2,1)}, bf16[32,4096]{1,0:T(8,128)(2,1)}, bf16[32,32]{1,0:T(8,128)(2,1)}, bf16[32,4096]{1,0:T(8,128)(2,1)}) custom-call(bf16[32,144,128]{2,1,0:T(8,128)(2,1)} %all_to_all.26.packed_ref), custom_call_target="tpu_custom_call" | custom-call | tf_op jit(solution)/shard_map/unspread/pallas_call | solution.py:399
  (1 shorter events, 0.0 us)
Async XLA Ops:
  2.7 29.7 %all-to-all-start = ((bf16[32,80,128]{2,1,0:T(8,128)(2,1)}), bf16[32,80,128]{2,1,0:T(8,128)(2,1)S(1)}, u32[]{:S(2)}, u32[]{:S(2)}) async-start(bf16[32,80,128]{2,1,0:T(8,128)(2,1)} %spread_keys.1), calls=%async_computation | async-start | bytes 1310720 | tf_op jit(solution)/shard_map/all_to_all | solution.py:413
  32.4 5.4 %copy-start = (bf16[32,80,128]{2,1,0:T(8,128)(2,1)}, bf16[32,80,128]{2,1,0:T(8,128)(2,1)S(1)}, u32[]{:S(2)}) copy-start(bf16[32,80,128]{2,1,0:T(8,128)(2,1)S(1)} %all-to-all-done.refs_0_.refs_1_) | copy-start | bytes 1966084
  32.4 26.5 %all-to-all-start.1 = ((bf16[32,96,128]{2,1,0:T(8,128)(2,1)}), bf16[32,96,128]{2,1,0:T(8,128)(2,1)S(1)}, u32[]{:S(2)}, u32[]{:S(2)}) async-start(bf16[32,96,128]{2,1,0:T(8,128)(2,1)} %spread_values.1), calls=%async_computation.1 | async-start | bytes 1572864 | tf_op jit(solution)/shard_map/all_to_all | solution.py:413
  58.9 7.2 %copy-start.1 = (bf16[32,96,128]{2,1,0:T(8,128)(2,1)}, bf16[32,96,128]{2,1,0:T(8,128)(2,1)S(1)}, u32[]{:S(2)}) copy-start(bf16[32,96,128]{2,1,0:T(8,128)(2,1)S(1)} %all-to-all-done.1.refs_1_.refs_2_) | copy-start | bytes 2359300
  59.8 17.5 %all-to-all-start.2 = ((f32[8,128,128]{2,1,0:T(8,128)}), f32[8,128,128]{2,1,0:T(8,128)S(1)}, u32[]{:S(2)}, u32[]{:S(2)}) async-start(f32[8,128,128]{2,1,0:T(8,128)} %broadcast_in_dim.11), calls=%async_computation.2 | async-start | bytes 1048576 | tf_op jit(solution)/shard_map/all_to_all | solution.py:416
  77.3 14.1 %copy-start.2 = (f32[8,128,128]{2,1,0:T(8,128)}, f32[8,128,128]{2,1,0:T(8,128)S(1)}, u32[]{:S(2)}) copy-start(f32[8,128,128]{2,1,0:T(8,128)S(1)} %all-to-all-done.2.refs_11_) | copy-start | bytes 1572868

commit v2 on v1

v2 whole, which is shorter than its diff:
```python
import jax
import jax.numpy as jnp
from jax import lax
from jax.experimental import pallas as pl
from jax.experimental.pallas import tpu as pltpu
from jax.sharding import Mesh, PartitionSpec as P

epsilon = 1e-06
bf16 = jnp.bfloat16
f32 = jnp.float32
CHUNK = 128
VMEM_BYTES = 32 << 20


def params(size=VMEM_BYTES):
    return pltpu.CompilerParams(vmem_limit_bytes=size)


def parts(value):
    high = value.astype(bf16)
    return (high, (value - high.astype(f32)).astype(bf16))


def beside(arrays, axis):
    return arrays[0] if len(arrays) == 1 else jnp.concatenate(arrays, axis)


def product(left, right, left_axis=1, right_axis=0):
    wide = right[0].shape[1 - right_axis]
    row = beside(right, 1 - right_axis)
    stacked = beside([row] * len(left), right_axis)
    lengthened = beside(left, left_axis)
    found = lax.dot_general(
        lengthened, stacked, (((left_axis,), (right_axis,)), ((), ())), preferred_element_type=f32
    )
    if len(right) == 1:
        return found
    return found[:, :wide] + found[:, wide:]


def indices():
    rows = lax.broadcasted_iota(jnp.int32, (CHUNK, CHUNK), 0)
    columns = lax.broadcasted_iota(jnp.int32, (CHUNK, CHUNK), 1)
    return rows, columns


def strength_of(packed):
    sources, half, lanes = packed.shape
    packed = packed.astype(f32)
    first = jnp.broadcast_to(packed[:, :, 0:1], (sources, half, lanes))
    second = jnp.broadcast_to(packed[:, :, lanes // 2 : lanes // 2 + 1], (sources, half, lanes))
    return jnp.concatenate([first, second], axis=1).reshape(sources * 2 * half, lanes)


def tree_levels(count):
    nodes = list(range(count))
    following = count
    found = []
    while len(nodes) > 1:
        above = []
        for left, right in zip(nodes[0::2], nodes[1::2]):
            found.append((following, left, right))
            above.append(following)
            following += 1
        nodes = above
    return found


GROUP = 8
SPAN = 32
SOURCES = CHUNK // SPAN


def rows_of(ref, piece, start, count):
    return ref[piece * SOURCES : (piece + 1) * SOURCES, start : start + count, :]


def chunk_of(ref, piece, place):
    return rows_of(ref, piece, place * SPAN, SPAN).reshape(CHUNK, ref.shape[2])


def key_terms(packed_ref, piece, causal_ones):
    key = chunk_of(packed_ref, piece, 0).astype(f32)
    decay = chunk_of(packed_ref, piece, 1)
    weight = strength_of(rows_of(packed_ref, piece, 5 * SPAN, SPAN // 2))
    gamma = jnp.dot(causal_ones, decay, preferred_element_type=f32)
    middle = gamma[CHUNK // 2 - 1 : CHUNK // 2]
    last = gamma[CHUNK - 1 : CHUNK]
    inverse = lax.rsqrt(jnp.sum(key * key, axis=1, keepdims=True) + epsilon)
    unit = key * inverse
    rise = jnp.exp(gamma - middle)
    fall = jnp.exp(middle - gamma)
    head = jnp.exp(gamma)
    tail = jnp.exp(last - gamma)
    return dict(
        unit=unit, inverse=inverse, weight=weight, rise=rise, fall=fall, head=head, tail=tail, fade=jnp.exp(last)
    )


def query_terms(packed_ref, piece):
    query = chunk_of(packed_ref, piece, 3).astype(f32)
    inverse = lax.rsqrt(jnp.sum(query * query, axis=1, keepdims=True) + epsilon)
    return query * inverse, inverse


def spread_kernel(key_ref, decay_ref, value_ref, query_ref, grad_ref, strength_ref, out_ref):
    for head in range(GROUP):
        lanes = slice(head * 128, (head + 1) * 128)
        for place, ref in enumerate((key_ref, decay_ref, value_ref, query_ref, grad_ref)):
            out_ref[head, place * SPAN : (place + 1) * SPAN, :] = ref[:, lanes]
    values = strength_ref[...].astype(f32)
    heads = lax.broadcasted_iota(jnp.int32, values.shape, 1)
    half = SPAN // 2
    early = lax.broadcasted_iota(jnp.int32, (half, 128), 1) < 64
    for head in range(GROUP):
        chosen = heads == pl.program_id(0) * GROUP + head
        column = jnp.sum(jnp.where(chosen, values, 0.0), axis=1, keepdims=True)
        packed = jnp.where(early, column[:half], column[half:])
        out_ref[head, 5 * SPAN : 5 * SPAN + half, :] = packed.astype(bf16)


def spread(key_in, log_decay, values_in, queries, d_out, strength):
    span, heads = strength.shape
    rows = 5 * SPAN + SPAN // 2
    wide = pl.BlockSpec((span, GROUP * 128), lambda step: (0, step))
    return pl.pallas_call(
        spread_kernel,
        grid=(heads // GROUP,),
        in_specs=[wide] * 5 + [pl.BlockSpec((span, heads), lambda step: (0, 0))],
        out_specs=pl.BlockSpec((GROUP, rows, 128), lambda step: (step, 0, 0)),
        out_shape=jax.ShapeDtypeStruct((heads, rows, 128), bf16),
        compiler_params=params(58 << 20),
        name="spread",
    )(key_in, log_decay, values_in, queries, d_out, strength)


def joined(value):
    return jnp.concatenate(parts(value), axis=1)


def halves(value):
    return (value[:, :CHUNK], value[:, CHUNK:])


SOLVE, INNER, WKEY, SCORES = range(4)


def local_kernel(
    pieces, blocks, place_ref, packed_ref, share_ref, maps_ref, wvalue_ref, transfer_ref, left_ref, right_ref
):
    rows, columns = indices()
    causal = rows >= columns
    causal_ones = jnp.where(causal, 1.0, 0.0).astype(bf16)
    strict = rows > columns
    eye = jnp.where(rows == columns, 1.0, 0.0)
    scale = CHUNK ** (-0.5)
    terms = [key_terms(packed_ref, piece, causal_ones) for piece in range(pieces)]
    systems = []
    solved = []
    pair = ((rows ^ columns) == 1) & strict
    for piece in range(pieces):
        t = terms[piece]
        fall_parts = parts(t["unit"] * t["fall"])
        inner = product(parts(t["unit"] * t["rise"]), fall_parts, 1, 1)
        inner = jnp.where(strict, inner, 0.0)
        maps_ref[INNER, piece] = joined(inner)
        query = query_terms(packed_ref, piece)[0] * (scale * t["rise"])
        scores = jnp.where(causal, product(parts(query), fall_parts, 1, 1), 0.0)
        maps_ref[SCORES, piece] = joined(scores)
        system = t["weight"] * inner
        systems.append(system)
        solved.append(eye - jnp.where(pair, system, 0.0))
    shift = 1
    while (1 << shift) < CHUNK:
        row_block = lax.shift_right_logical(rows, shift)
        column_block = lax.shift_right_logical(columns, shift)
        corner = (row_block == column_block + 1) & ((row_block & 1) == 1)
        for piece in range(pieces):
            inverse = parts(solved[piece])
            block = parts(jnp.where(corner, systems[piece], 0.0))
            between = product(parts(product(inverse, block)), inverse)
            solved[piece] = solved[piece] - between
        shift += 1
    transfers = []
    offsets = []
    injects = []
    for piece in range(pieces):
        t = terms[piece]
        solve = parts(solved[piece])
        maps_ref[SOLVE, piece] = jnp.concatenate(solve, axis=1)
        value = chunk_of(packed_ref, piece, 2).astype(f32)
        wkey = parts(product(solve, parts(t["weight"] * (t["unit"] * t["head"]))))
        maps_ref[WKEY, piece] = jnp.concatenate(wkey, axis=1)
        wvalue = product(solve, parts(t["weight"] * value))
        wvalue_ref[piece] = wvalue
        tail = parts(t["unit"] * t["tail"])
        transfers.append(eye * t["fade"] - product(tail, wkey, 0, 0))
        offsets.append(product(tail, parts(wvalue), 0, 0))
        query = query_terms(packed_ref, piece)[0] * (scale * t["head"])
        reach = query - product(halves(maps_ref[SCORES, piece]), wkey)
        injects.append(product(parts(reach), (chunk_of(packed_ref, piece, 4),), 0, 0))
    for parent, left, right in tree_levels(pieces):
        transfer_left = parts(transfers[left])
        transfer_right = parts(transfers[right])
        transfer_ref[left] = jnp.concatenate(transfer_left, axis=1)
        transfer_ref[right] = jnp.concatenate(transfer_right, axis=1)
        left_ref[parent - pieces] = offsets[left]
        right_ref[parent - pieces] = injects[right]
        transfers.append(product(transfer_right, transfer_left))
        offsets.append(product(transfer_right, parts(offsets[left])) + offsets[right])
        injects.append(injects[left] + product(transfer_left, parts(injects[right]), 0, 0))
    place = place_ref[0]
    for block in range(blocks):
        share_ref[block, :CHUNK] = transfers[-1]
        share_ref[block, CHUNK:] = jnp.where(block > place, offsets[-1], injects[-1])


def saved_shapes(pieces):
    return (
        ((4, pieces, CHUNK, 2 * CHUNK), bf16),
        ((pieces, CHUNK, CHUNK), f32),
        ((2 * pieces - 2, CHUNK, 2 * CHUNK), bf16),
        ((pieces - 1, CHUNK, CHUNK), f32),
        ((pieces - 1, CHUNK, CHUNK), f32),
    )


def local_stage(place, blocks, packed):
    pieces = packed.shape[0] * SPAN // CHUNK
    saved = saved_shapes(pieces)

    def body(*refs):
        local_kernel(pieces, blocks, *refs)

    share, *found = pl.pallas_call(
        body,
        in_specs=[pl.BlockSpec(memory_space=pltpu.SMEM), pl.BlockSpec(memory_space=pltpu.VMEM)],
        out_shape=[jax.ShapeDtypeStruct((blocks, 2 * CHUNK, CHUNK), f32)]
        + [jax.ShapeDtypeStruct(shape, dtype) for shape, dtype in saved],
        compiler_params=params(),
        name="local_stage",
    )(place, packed)
    return share, found


def grads_kernel(
    pieces,
    blocks,
    place_ref,
    packed_ref,
    far_ref,
    maps_ref,
    wvalue_ref,
    transfer_ref,
    left_ref,
    right_ref,
    out_ref,
    state_ref,
    cot_ref,
):
    rows, columns = indices()
    causal = rows >= columns
    strict = rows > columns
    causal_ones = jnp.where(causal, 1.0, 0.0).astype(bf16)
    reverse_ones = jnp.where(rows <= columns, 1.0, 0.0).astype(bf16)
    sum_ones = jnp.ones((16, CHUNK), bf16)
    early = lax.broadcasted_iota(jnp.int32, (SOURCES, SPAN // 2, CHUNK), 2) < CHUNK // 2
    scale = CHUNK ** (-0.5)
    place = place_ref[0]
    state = jnp.where(place > 0, far_ref[0, CHUNK:], 0.0)
    cot = jnp.where(place < blocks - 1, far_ref[blocks - 1, CHUNK:], 0.0)
    for step in range(1, blocks - 1):
        back = blocks - 1 - step
        moved = product(parts(far_ref[step, :CHUNK]), parts(state)) + far_ref[step, CHUNK:]
        returned = product(parts(far_ref[back, :CHUNK]), parts(cot), 0, 0) + far_ref[back, CHUNK:]
        state = jnp.where(place > step, moved, state)
        cot = jnp.where(place < back, returned, cot)
    state_ref[2 * pieces - 2] = state
    cot_ref[2 * pieces - 2] = cot
    for parent, left, right in reversed(tree_levels(pieces)):
        state = state_ref[parent]
        cot = cot_ref[parent]
        state_ref[left] = state
        state_ref[right] = product(halves(transfer_ref[left]), parts(state)) + left_ref[parent - pieces]
        cot_ref[right] = cot
        cot_ref[left] = product(halves(transfer_ref[right]), parts(cot), 0, 0) + right_ref[parent - pieces]
    for piece in range(pieces):
        t = key_terms(packed_ref, piece, causal_ones)
        query_one, query_inverse = query_terms(packed_ref, piece)
        query = query_one * scale
        value = chunk_of(packed_ref, piece, 2).astype(f32)
        grad = chunk_of(packed_ref, piece, 4)
        state = state_ref[piece]
        cot = cot_ref[piece]
        state_parts = parts(state)
        cot_parts = parts(cot)
        unit = t["unit"]
        key_rise = unit * t["rise"]
        key_fall = unit * t["fall"]
        key_head = unit * t["head"]
        key_tail = unit * t["tail"]
        update = wvalue_ref[piece] - product(halves(maps_ref[WKEY, piece]), state_parts)
        update_parts = parts(update)
        d_update = product(halves(maps_ref[SCORES, piece]), (grad,), 0, 0) + product(parts(key_tail), cot_parts)
        d_right = product(halves(maps_ref[SOLVE, piece]), parts(d_update), 0, 0)
        d_value = t["weight"] * d_right
        missed = value - product(parts(key_head), state_parts)
        missed = missed - product(halves(maps_ref[INNER, piece]), update_parts)
        d_weight = jnp.sum(d_right * missed, axis=1, keepdims=True)
        d_value_parts = parts(d_value)
        d_query_head = product((grad,), state_parts, 1, 1)
        d_key_head = -product(d_value_parts, state_parts, 1, 1)
        d_key_tail = product(update_parts, cot_parts, 1, 1)
        d_scores = jnp.where(causal, product((grad,), update_parts, 1, 1), 0.0)
        d_inner = jnp.where(strict, -product(d_value_parts, update_parts, 1, 1), 0.0)
        d_scores_parts = parts(d_scores)
        d_inner_parts = parts(d_inner)
        fall_parts = parts(key_fall)
        query_rise = query * t["rise"]
        d_query_rise = product(d_scores_parts, fall_parts)
        d_key_rise = product(d_inner_parts, fall_parts)
        d_key_fall = product(d_scores_parts, parts(query_rise), 0, 0) + product(
            d_inner_parts, parts(key_rise), 0, 0
        )
        d_query_unit = d_query_rise * t["rise"] + d_query_head * t["head"]
        up = d_key_rise * t["rise"] + d_key_head * t["head"]
        tail_term = d_key_tail * t["tail"]
        down = d_key_fall * t["fall"] + tail_term
        d_key_unit = up + down
        d_gamma = query * d_query_unit + unit * (up - down)
        faded = cot * state
        faded_high, faded_low = parts(faded)
        faded_rest = (faded - faded_high.astype(f32) - faded_low.astype(f32)).astype(bf16)
        d_fade = product((sum_ones,), (faded_high, faded_low), 1, 1) + product(
            (sum_ones,), (faded_rest,), 1, 1
        )
        d_last = jnp.sum(unit * tail_term, axis=0, keepdims=True) + d_fade[0:1] * t["fade"]
        gamma_high, gamma_low = parts(d_gamma)
        gamma_rest = (d_gamma - gamma_high.astype(f32) - gamma_low.astype(f32)).astype(bf16)
        d_decay = (
            product((reverse_ones,), (gamma_high, gamma_low))
            + product((reverse_ones,), (gamma_rest,))
            + d_last
        )
        d_query = (scale * query_inverse) * (
            d_query_unit - query_one * jnp.sum(query_one * d_query_unit, axis=1, keepdims=True)
        )
        d_key = t["inverse"] * (d_key_unit - unit * jnp.sum(unit * d_key_unit, axis=1, keepdims=True))
        span = slice(piece * SOURCES, (piece + 1) * SOURCES)

        def shaped(array):
            return array.astype(bf16).reshape(SOURCES, SPAN, CHUNK)

        out_ref[span, 0:32, :] = shaped(d_query)
        out_ref[span, 32:64, :] = shaped(d_key)
        out_ref[span, 64:96, :] = shaped(d_value)
        out_ref[span, 96:128, :] = shaped(d_decay)
        weights = jnp.broadcast_to(d_weight, (CHUNK, CHUNK)).reshape(SOURCES, SPAN, CHUNK)
        out_ref[span, 128:144, :] = jnp.where(early, weights[:, :16], weights[:, 16:]).astype(bf16)


def grads_stage(place, packed, far, saved):
    sources = packed.shape[0]
    pieces = sources * SPAN // CHUNK
    blocks = far.shape[0]

    def body(*refs):
        grads_kernel(pieces, blocks, *refs)

    return pl.pallas_call(
        body,
        in_specs=[pl.BlockSpec(memory_space=pltpu.SMEM)]
        + [pl.BlockSpec(memory_space=pltpu.VMEM)] * (2 + len(saved)),
        out_specs=pl.BlockSpec(memory_space=pltpu.VMEM),
        out_shape=jax.ShapeDtypeStruct((sources, 4 * SPAN + SPAN // 2, CHUNK), bf16),
        scratch_shapes=[pltpu.VMEM((2 * pieces - 1, CHUNK, CHUNK), f32)] * 2,
        compiler_params=params(),
        name="grads_stage",
    )(place, packed, far, *saved)


def unspread_kernel(packed_ref, query_ref, key_ref, value_ref, decay_ref, strength_ref):
    for head in range(GROUP):
        lanes = slice(head * 128, (head + 1) * 128)
        for place, ref in enumerate((query_ref, key_ref, value_ref, decay_ref)):
            ref[:, lanes] = packed_ref[head, place * SPAN : (place + 1) * SPAN, :]
    first = pl.program_id(0) * GROUP
    place = lax.broadcasted_iota(jnp.int32, (SPAN, 128), 1)
    total = jnp.zeros((SPAN, 128), f32)
    for head in range(GROUP):
        column = strength_of(packed_ref[head : head + 1, 4 * SPAN : 4 * SPAN + SPAN // 2, :])
        total = jnp.where(place == first + head, column, total)
    chosen = (place >= first) & (place < first + GROUP)
    heads = strength_ref.shape[1]
    before = strength_ref[...].astype(f32)
    strength_ref[...] = jnp.where(chosen[:, :heads], total[:, :heads], before).astype(bf16)


def unspread(packed, span):
    heads, rows, _ = packed.shape
    wide = jax.ShapeDtypeStruct((span, heads * 128), bf16)
    spec = pl.BlockSpec((span, GROUP * 128), lambda step: (0, step))
    return pl.pallas_call(
        unspread_kernel,
        grid=(heads // GROUP,),
        in_specs=[pl.BlockSpec((GROUP, rows, 128), lambda step: (step, 0, 0))],
        out_specs=(spec, spec, spec, spec, pl.BlockSpec((span, heads), lambda step: (0, 0))),
        out_shape=(wide, wide, wide, wide, jax.ShapeDtypeStruct((span, heads), bf16)),
        compiler_params=params(),
        name="unspread",
    )(packed)


def per_device(queries, key_in, values_in, strength, log_decay, d_out):
    blocks = lax.axis_size("block")
    place = lax.axis_index("block").astype(jnp.int32).reshape(1)

    def swap(array):
        return lax.all_to_all(array, ("near", "head"), 0, 0, tiled=True)

    packed = swap(spread(key_in, log_decay, values_in, queries, d_out, strength))
    share, saved = local_stage(place, blocks, packed)
    far = lax.all_to_all(share, "block", 0, 0, tiled=True)
    d_packed = swap(grads_stage(place, packed, far, saved))
    d_query, d_key, d_value, d_decay, d_strength = unspread(d_packed, queries.shape[0])
    return d_query, d_key, d_value, d_strength, d_decay


def solution(mesh):
    heads_axis = mesh.shape["head"]
    near = 32 // heads_axis
    wide = Mesh(mesh.devices.reshape(-1, near, heads_axis), ("block", "near", "head"))
    spec = P(("block", "near", "head"), None)
    return jax.shard_map(
        per_device, mesh=wide, in_specs=(spec,) * 6, out_specs=(spec,) * 5, check_vma=False
    )
```

time: 147 us -> 129 us (0.88)
  Pallas kernels: 32.6 us -> 20.9 us
  starting transfers between devices: 22.8 us -> 11.1 us
  blocking collectives: 52.9 us -> 61.6 us
  local copies, waits for them, and re-layouts: 2.6 us -> 0 us
    all_to_all x1, blocking collectives: 14.1 us -> 23.6 us  [per_device(): far = lax.all_to_all(share, 'block', 0, 0, tiled=True)]
    pallas_call x5 -> x3, Pallas kernels: 19.2 us -> 11.8 us  [the longest x1 6.55 us: local_stage(): pl.pallas_call(body, in_specs=[pl.BlockSpec(memory_space=pltpu.SMEM), pl....]
    all_to_all x1 -> x0, starting transfers between devices: 6.36 us -> none  [share(): return lax.all_to_all(array, 'block', 0, 0, tiled=True)]
    all_to_all x2 -> x1, starting transfers between devices: 16.4 us -> 11.1 us  [swap(): return lax.all_to_all(array, ('near', 'head'), 0, 0, tiled=True)]
    pallas_call x1, Pallas kernels: 13.5 us -> 9.17 us  [grads_stage(): pl.pallas_call(body, in_specs=[pl.BlockSpec(memory_space=pltpu.SMEM)] + [...]
    all_to_all x2 -> x1, waiting for transfers between devices: 31.2 us -> 34.6 us  [swap(): return lax.all_to_all(array, ('near', 'head'), 0, 0, tiled=True)]
    all_to_all x1 -> x0, waiting for transfers between devices: 3.06 us -> none  [share(): return lax.all_to_all(array, 'block', 0, 0, tiled=True)]
    squeeze x2 -> x0, local copies, waits for them, and re-layouts: 1.72 us -> none  [the longest x1 0.88 us: per_device(): far = share(jnp.where(later, offset[-1], inject[-1]))]
  transfers between devices with their start and end apart: 3 -> 1, of which waited for: 3 -> 1; matrix products, arithmetic and copies ran while one was open for 1% -> 0% of each run, Pallas kernels for 10% -> 0%
where the time goes in v2:
time: 129 us
  blocking collectives  61.6 us (48%)
  waiting for transfers between devices  34.6 us (27%)
  Pallas kernels  20.9 us (16%)
  starting transfers between devices  11.1 us (9%)
    all_to_all x1, blocking collectives, swap(): return lax.all_to_all(array, ('near', 'head'), 0, 0, tiled=True)  38 us
    all_to_all x1, waiting for transfers between devices, swap(): return lax.all_to_all(array, ('near', 'head'), 0, 0, tiled=True)  34.6 us
    all_to_all x1, blocking collectives, per_device(): far = lax.all_to_all(share, 'block', 0, 0, tiled=True)  23.6 us
    all_to_all x1, starting transfers between devices, swap(): return lax.all_to_all(array, ('near', 'head'), 0, 0, tiled=True)  11.1 us
    pallas_call x1, Pallas kernels, grads_stage(): pl.pallas_call(body, in_specs=[pl.BlockSpec(memory_space=pltpu.SMEM)] + [...  9.17 us
    pallas_call x1, Pallas kernels, local_stage(): pl.pallas_call(body, in_specs=[pl.BlockSpec(memory_space=pltpu.SMEM), pl....  6.55 us
    pallas_call x1, Pallas kernels, spread(): pl.pallas_call(spread_kernel, grid=(heads // GROUP,), in_specs=[wide] * 5...  3.68 us
  transfers between devices with their start and end apart: 1, of which 1 were waited for; matrix products, arithmetic and copies ran while one was open for 0% of the time, Pallas kernels for 0%

profile of v2, /device:TPU:1, one launch (start us, length us, event | category | flops | bytes accessed | tf_op | source)
XLA Modules:
  0.0 129.0 jit_solution(5449366990148525601)
XLA Ops:
  0.6 3.7 %spread.1 = bf16[32,176,128]{2,1,0:T(8,128)(2,1)} custom-call(bf16[32,4096]{1,0:T(8,128)(2,1)} %key_ref.1, bf16[32,4096]{1,0:T(8,128)(2,1)} %decay_ref.1, bf16[32,4096]{1,0:T(8,128)(2,1)} %value_ref.1, bf16[32,4096]{1,0:T(8,128)(2,1)} %query_ref.1, bf16[32,4096]{1,0:T(8,128)(2,1)} %grad_ref.1, bf16[32,32]{1,0:T(8,128)(2,1)} %strength_ref.1), custom_call_target="tpu_custom_call" | custom-call | tf_op jit(solution)/shard_map/spread/pallas_call | solution.py:126
  4.3 11.1 %all-to-all-start = ((bf16[32,176,128]{2,1,0:T(8,128)(2,1)}), bf16[32,176,128]{2,1,0:T(8,128)(2,1)S(1)}, u32[]{:S(2)}, u32[]{:S(2)}) async-start(bf16[32,176,128]{2,1,0:T(8,128)(2,1)} %spread.1), calls=%async_computation | async-start | bytes 2883584 | tf_op jit(solution)/shard_map/all_to_all | solution.py:419
  15.4 34.6 %all-to-all-done.refs_1_ = bf16[32,176,128]{2,1,0:T(8,128)(2,1)S(1)} async-done(((bf16[32,176,128]{2,1,0:T(8,128)(2,1)}), bf16[32,176,128]{2,1,0:T(8,128)(2,1)S(1)}, u32[]{:S(2)}, u32[]{:S(2)}) %all-to-all-start) | async-done | bytes 1441824 | tf_op jit(solution)/shard_map/all_to_all | solution.py:419
  49.9 6.6 %local_stage.1 = (f32[8,256,128]{2,1,0:T(8,128)S(1)}, bf16[4,8,128,256]{3,2,1,0:T(8,128)(2,1)S(1)}, f32[8,128,128]{2,1,0:T(8,128)S(1)}, bf16[14,128,256]{2,1,0:T...) custom-call(s32[1]{0:T(128)} %bitcast.refs_0_, bf16[32,176,128]{2,1,0:T(8,128)(2,1)S(1)} %all-to-all-done.refs_1_), custom_call_target="tpu_custom_call" | custom-call | tf_op jit(solution)/shard_map/local_stage/pallas_call | solution.py:235
  56.5 23.6 %all_to_all.15.refs_2_ = f32[8,256,128]{2,1,0:T(8,128)S(1)} all-to-all(f32[8,256,128]{2,1,0:T(8,128)S(1)} %get-tuple-element.16), channel_id=1, replica_groups=mesh['block'=8,'near'=4,'head'=8] {'block'}, dimensions={0} | all-to-all | bytes 2097152 | tf_op jit(solution)/shard_map/all_to_all | solution.py:423
  80.1 9.2 %grads_stage.1 = bf16[32,144,128]{2,1,0:T(8,128)(2,1)S(1)} custom-call(s32[1]{0:T(128)} %bitcast.refs_0_, bf16[32,176,128]{2,1,0:T(8,128)(2,1)S(1)} %all-to-all-done.refs_1_, f32[8,256,128]{2,1,0:T(8,128)S(1)} %all_to_all.15.refs_2_, bf16[4,8,128,256]{3,2,1,0:T(8,128)(2,1)S(1)} %get-tuple-element.17.refs_3_, f32[8,128,128]{2,1,0:T(8,128)S(1)} %get-tuple-element.18.refs_4_, ...), custom_call_target="tpu_custom_call" | custom-call | tf_op jit(solution)/shard_map/grads_stage/pallas_call | solution.py:370
  89.3 38.0 %all_to_all.16.packed_ref = bf16[32,144,128]{2,1,0:T(8,128)(2,1)S(1)} all-to-all(bf16[32,144,128]{2,1,0:T(8,128)(2,1)S(1)} %grads_stage.1), channel_id=1, replica_groups=mesh['block'=8,'near'=4,'head'=8] {'near','head'}, dimensions={0} | all-to-all | bytes 2359296 | tf_op jit(solution)/shard_map/all_to_all | solution.py:419
  127.3 1.5 %unspread.1 = (bf16[32,4096]{1,0:T(8,128)(2,1)}, bf16[32,4096]{1,0:T(8,128)(2,1)}, bf16[32,4096]{1,0:T(8,128)(2,1)}, bf16[32,4096]{1,0:T(8,128)(2,1)}, bf16[32,32]{1,0:T(8,128)(2,1)}) custom-call(bf16[32,144,128]{2,1,0:T(8,128)(2,1)S(1)} %all_to_all.16.packed_ref), custom_call_target="tpu_custom_call" | custom-call | tf_op jit(solution)/shard_map/unspread/pallas_call | solution.py:403
Async XLA Ops:
  4.3 45.6 %all-to-all-start = ((bf16[32,176,128]{2,1,0:T(8,128)(2,1)}), bf16[32,176,128]{2,1,0:T(8,128)(2,1)S(1)}, u32[]{:S(2)}, u32[]{:S(2)}) async-start(bf16[32,176,128]{2,1,0:T(8,128)(2,1)} %spread.1), calls=%async_computation | async-start | bytes 2883584 | tf_op jit(solution)/shard_map/all_to_all | solution.py:419

commit v3 on v2

--- a/solution.py
+++ b/solution.py
@@ -45,11 +45,33 @@
 
 
 def strength_of(packed):
-    sources, half, lanes = packed.shape
+    sources, rows, lanes = packed.shape
     packed = packed.astype(f32)
-    first = jnp.broadcast_to(packed[:, :, 0:1], (sources, half, lanes))
-    second = jnp.broadcast_to(packed[:, :, lanes // 2 : lanes // 2 + 1], (sources, half, lanes))
-    return jnp.concatenate([first, second], axis=1).reshape(sources * 2 * half, lanes)
+    found = []
+    for place in range(FOLD):
+        lane = place * (lanes // FOLD)
+        found.append(jnp.broadcast_to(packed[:, :, lane : lane + 1], (sources, rows, lanes)))
+    return jnp.concatenate(found, axis=1).reshape(sources * FOLD * rows, lanes)
+
+
+def strength_folded(values):
+    sources, rows, _ = values.shape
+    rows = rows // FOLD
+    lane = lax.broadcasted_iota(jnp.int32, (sources, rows, 128), 2)
+    found = jnp.broadcast_to(values[:, :rows], (sources, rows, 128))
+    for place in range(1, FOLD):
+        found = jnp.where(lane >= place * (128 // FOLD), values[:, place * rows : (place + 1) * rows], found)
+    return found.astype(bf16)
+
+
+def in_step(bodies):
+    bodies = list(bodies)
+    while bodies:
+        running = []
+        for body in bodies:
+            if next(body, True) is None:
+                running.append(body)
+        bodies = running
 
 
 def tree_levels(count):
@@ -66,7 +88,8 @@
     return found
 
 
-GROUP = 8
+GROUP = 16
+FOLD = 4
 SPAN = 32
 SOURCES = CHUNK // SPAN
 
@@ -82,7 +105,7 @@
 def key_terms(packed_ref, piece, causal_ones):
     key = chunk_of(packed_ref, piece, 0).astype(f32)
     decay = chunk_of(packed_ref, piece, 1)
-    weight = strength_of(rows_of(packed_ref, piece, 5 * SPAN, SPAN // 2))
+    weight = strength_of(rows_of(packed_ref, piece, 5 * SPAN, SPAN // FOLD))
     gamma = jnp.dot(causal_ones, decay, preferred_element_type=f32)
     middle = gamma[CHUNK // 2 - 1 : CHUNK // 2]
     last = gamma[CHUNK - 1 : CHUNK]
@@ -110,18 +133,15 @@
             out_ref[head, place * SPAN : (place + 1) * SPAN, :] = ref[:, lanes]
     values = strength_ref[...].astype(f32)
     heads = lax.broadcasted_iota(jnp.int32, values.shape, 1)
-    half = SPAN // 2
-    early = lax.broadcasted_iota(jnp.int32, (half, 128), 1) < 64
     for head in range(GROUP):
         chosen = heads == pl.program_id(0) * GROUP + head
         column = jnp.sum(jnp.where(chosen, values, 0.0), axis=1, keepdims=True)
-        packed = jnp.where(early, column[:half], column[half:])
-        out_ref[head, 5 * SPAN : 5 * SPAN + half, :] = packed.astype(bf16)
+        out_ref[head : head + 1, 5 * SPAN :, :] = strength_folded(column[None])
 
 
 def spread(key_in, log_decay, values_in, queries, d_out, strength):
     span, heads = strength.shape
-    rows = 5 * SPAN + SPAN // 2
+    rows = 5 * SPAN + SPAN // FOLD
     wide = pl.BlockSpec((span, GROUP * 128), lambda step: (0, step))
     return pl.pallas_call(
         spread_kernel,
@@ -154,51 +174,67 @@
     strict = rows > columns
     eye = jnp.where(rows == columns, 1.0, 0.0)
     scale = CHUNK ** (-0.5)
-    terms = [key_terms(packed_ref, piece, causal_ones) for piece in range(pieces)]
-    systems = []
-    solved = []
+    terms = [None] * pieces
+    systems = [None] * pieces
+    solved = [None] * pieces
     pair = ((rows ^ columns) == 1) & strict
-    for piece in range(pieces):
-        t = terms[piece]
+
+    def begin(piece):
+        t = terms[piece] = key_terms(packed_ref, piece, causal_ones)
+        query = query_terms(packed_ref, piece)[0] * scale
+        yield
         fall_parts = parts(t["unit"] * t["fall"])
         inner = product(parts(t["unit"] * t["rise"]), fall_parts, 1, 1)
+        yield
+        scores = product(parts(query * t["rise"]), fall_parts, 1, 1)
+        yield
         inner = jnp.where(strict, inner, 0.0)
         maps_ref[INNER, piece] = joined(inner)
-        query = query_terms(packed_ref, piece)[0] * (scale * t["rise"])
-        scores = jnp.where(causal, product(parts(query), fall_parts, 1, 1), 0.0)
-        maps_ref[SCORES, piece] = joined(scores)
-        system = t["weight"] * inner
-        systems.append(system)
-        solved.append(eye - jnp.where(pair, system, 0.0))
+        systems[piece] = t["weight"] * inner
+        solved[piece] = eye - jnp.where(pair, systems[piece], 0.0)
+        yield
+        maps_ref[SCORES, piece] = joined(jnp.where(causal, scores, 0.0))
+
+    in_step(begin(piece) for piece in range(pieces))
     shift = 1
     while (1 << shift) < CHUNK:
         row_block = lax.shift_right_logical(rows, shift)
         column_block = lax.shift_right_logical(columns, shift)
         corner = (row_block == column_block + 1) & ((row_block & 1) == 1)
-        for piece in range(pieces):
+
+        def widen(piece):
             inverse = parts(solved[piece])
-            block = parts(jnp.where(corner, systems[piece], 0.0))
-            between = product(parts(product(inverse, block)), inverse)
-            solved[piece] = solved[piece] - between
+            between = product(inverse, parts(jnp.where(corner, systems[piece], 0.0)))
+            yield
+            solved[piece] = solved[piece] - product(parts(between), inverse)
+
+        in_step(widen(piece) for piece in range(pieces))
         shift += 1
-    transfers = []
-    offsets = []
-    injects = []
-    for piece in range(pieces):
+    transfers = [None] * pieces
+    offsets = [None] * pieces
+    injects = [None] * pieces
+
+    def end(piece):
         t = terms[piece]
         solve = parts(solved[piece])
         maps_ref[SOLVE, piece] = jnp.concatenate(solve, axis=1)
-        value = chunk_of(packed_ref, piece, 2).astype(f32)
         wkey = parts(product(solve, parts(t["weight"] * (t["unit"] * t["head"]))))
+        yield
         maps_ref[WKEY, piece] = jnp.concatenate(wkey, axis=1)
-        wvalue = product(solve, parts(t["weight"] * value))
+        wvalue = product(solve, parts(t["weight"] * chunk_of(packed_ref, piece, 2).astype(f32)))
+        yield
         wvalue_ref[piece] = wvalue
         tail = parts(t["unit"] * t["tail"])
-        transfers.append(eye * t["fade"] - product(tail, wkey, 0, 0))
-        offsets.append(product(tail, parts(wvalue), 0, 0))
+        transfers[piece] = eye * t["fade"] - product(tail, wkey, 0, 0)
+        yield
+        offsets[piece] = product(tail, parts(wvalue), 0, 0)
+        yield
         query = query_terms(packed_ref, piece)[0] * (scale * t["head"])
         reach = query - product(halves(maps_ref[SCORES, piece]), wkey)
-        injects.append(product(parts(reach), (chunk_of(packed_ref, piece, 4),), 0, 0))
+        yield
+        injects[piece] = product(parts(reach), (chunk_of(packed_ref, piece, 4),), 0, 0)
+
+    in_step(end(piece) for piece in range(pieces))
     for parent, left, right in tree_levels(pieces):
         transfer_left = parts(transfers[left])
         transfer_right = parts(transfers[right])
@@ -264,7 +300,6 @@
     causal_ones = jnp.where(causal, 1.0, 0.0).astype(bf16)
     reverse_ones = jnp.where(rows <= columns, 1.0, 0.0).astype(bf16)
     sum_ones = jnp.ones((16, CHUNK), bf16)
-    early = lax.broadcasted_iota(jnp.int32, (SOURCES, SPAN // 2, CHUNK), 2) < CHUNK // 2
     scale = CHUNK ** (-0.5)
     place = place_ref[0]
     state = jnp.where(place > 0, far_ref[0, CHUNK:], 0.0)
@@ -284,12 +319,13 @@
         state_ref[right] = product(halves(transfer_ref[left]), parts(state)) + left_ref[parent - pieces]
         cot_ref[right] = cot
         cot_ref[left] = product(halves(transfer_ref[right]), parts(cot), 0, 0) + right_ref[parent - pieces]
-    for piece in range(pieces):
+    def work(piece):
         t = key_terms(packed_ref, piece, causal_ones)
         query_one, query_inverse = query_terms(packed_ref, piece)
         query = query_one * scale
         value = chunk_of(packed_ref, piece, 2).astype(f32)
         grad = chunk_of(packed_ref, piece, 4)
+        yield
         state = state_ref[piece]
         cot = cot_ref[piece]
         state_parts = parts(state)
@@ -300,28 +336,35 @@
         key_head = unit * t["head"]
         key_tail = unit * t["tail"]
         update = wvalue_ref[piece] - product(halves(maps_ref[WKEY, piece]), state_parts)
+        yield
         update_parts = parts(update)
         d_update = product(halves(maps_ref[SCORES, piece]), (grad,), 0, 0) + product(parts(key_tail), cot_parts)
+        yield
         d_right = product(halves(maps_ref[SOLVE, piece]), parts(d_update), 0, 0)
         d_value = t["weight"] * d_right
         missed = value - product(parts(key_head), state_parts)
+        yield
         missed = missed - product(halves(maps_ref[INNER, piece]), update_parts)
         d_weight = jnp.sum(d_right * missed, axis=1, keepdims=True)
         d_value_parts = parts(d_value)
         d_query_head = product((grad,), state_parts, 1, 1)
+        yield
         d_key_head = -product(d_value_parts, state_parts, 1, 1)
         d_key_tail = product(update_parts, cot_parts, 1, 1)
         d_scores = jnp.where(causal, product((grad,), update_parts, 1, 1), 0.0)
         d_inner = jnp.where(strict, -product(d_value_parts, update_parts, 1, 1), 0.0)
+        yield
         d_scores_parts = parts(d_scores)
         d_inner_parts = parts(d_inner)
         fall_parts = parts(key_fall)
         query_rise = query * t["rise"]
         d_query_rise = product(d_scores_parts, fall_parts)
         d_key_rise = product(d_inner_parts, fall_parts)
+        yield
         d_key_fall = product(d_scores_parts, parts(query_rise), 0, 0) + product(
             d_inner_parts, parts(key_rise), 0, 0
         )
+        yield
         d_query_unit = d_query_rise * t["rise"] + d_query_head * t["head"]
         up = d_key_rise * t["rise"] + d_key_head * t["head"]
         tail_term = d_key_tail * t["tail"]
@@ -331,17 +374,20 @@
         faded = cot * state
         faded_high, faded_low = parts(faded)
         faded_rest = (faded - faded_high.astype(f32) - faded_low.astype(f32)).astype(bf16)
+        yield
         d_fade = product((sum_ones,), (faded_high, faded_low), 1, 1) + product(
             (sum_ones,), (faded_rest,), 1, 1
         )
         d_last = jnp.sum(unit * tail_term, axis=0, keepdims=True) + d_fade[0:1] * t["fade"]
         gamma_high, gamma_low = parts(d_gamma)
         gamma_rest = (d_gamma - gamma_high.astype(f32) - gamma_low.astype(f32)).astype(bf16)
+        yield
         d_decay = (
             product((reverse_ones,), (gamma_high, gamma_low))
             + product((reverse_ones,), (gamma_rest,))
             + d_last
         )
+        yield
         d_query = (scale * query_inverse) * (
             d_query_unit - query_one * jnp.sum(query_one * d_query_unit, axis=1, keepdims=True)
         )
@@ -356,7 +402,9 @@
         out_ref[span, 64:96, :] = shaped(d_value)
         out_ref[span, 96:128, :] = shaped(d_decay)
         weights = jnp.broadcast_to(d_weight, (CHUNK, CHUNK)).reshape(SOURCES, SPAN, CHUNK)
-        out_ref[span, 128:144, :] = jnp.where(early, weights[:, :16], weights[:, 16:]).astype(bf16)
+        out_ref[span, 4 * SPAN :, :] = strength_folded(weights)
+
+    in_step(work(piece) for piece in range(pieces))
 
 
 def grads_stage(place, packed, far, saved):
@@ -372,7 +420,7 @@
         in_specs=[pl.BlockSpec(memory_space=pltpu.SMEM)]
         + [pl.BlockSpec(memory_space=pltpu.VMEM)] * (2 + len(saved)),
         out_specs=pl.BlockSpec(memory_space=pltpu.VMEM),
-        out_shape=jax.ShapeDtypeStruct((sources, 4 * SPAN + SPAN // 2, CHUNK), bf16),
+        out_shape=jax.ShapeDtypeStruct((sources, 4 * SPAN + SPAN // FOLD, CHUNK), bf16),
         scratch_shapes=[pltpu.VMEM((2 * pieces - 1, CHUNK, CHUNK), f32)] * 2,
         compiler_params=params(),
         name="grads_stage",
@@ -388,7 +436,7 @@
     place = lax.broadcasted_iota(jnp.int32, (SPAN, 128), 1)
     total = jnp.zeros((SPAN, 128), f32)
     for head in range(GROUP):
-        column = strength_of(packed_ref[head : head + 1, 4 * SPAN : 4 * SPAN + SPAN // 2, :])
+        column = strength_of(packed_ref[head : head + 1, 4 * SPAN :, :])
         total = jnp.where(place == first + head, column, total)
     chosen = (place >= first) & (place < first + GROUP)
     heads = strength_ref.shape[1]

time: 129 us -> 120 us (0.930)
  Pallas kernels: 20.9 us -> 13.6 us
  waiting for transfers between devices: 34.6 us -> 33.2 us
    pallas_call x1, Pallas kernels: 9.17 us -> 5.34 us  [grads_stage(): pl.pallas_call(body, in_specs=[pl.BlockSpec(memory_space=pltpu.SMEM)] + [...]
    pallas_call x1, Pallas kernels: 6.55 us -> 4.86 us  [local_stage(): pl.pallas_call(body, in_specs=[pl.BlockSpec(memory_space=pltpu.SMEM), pl....]
    all_to_all x1, waiting for transfers between devices: 34.6 us -> 33.2 us  [swap(): return lax.all_to_all(array, ('near', 'head'), 0, 0, tiled=True)]
where the time goes in v3:
time: 120 us; the launch traced here: 119 us
  blocking collectives  60.7 us (51%)
  waiting for transfers between devices  33.2 us (28%)
  Pallas kernels  13.6 us (11%)
  starting transfers between devices  11.1 us (9%)
    all_to_all x1, blocking collectives, swap(): return lax.all_to_all(array, ('near', 'head'), 0, 0, tiled=True)  37.4 us
    all_to_all x1, waiting for transfers between devices, swap(): return lax.all_to_all(array, ('near', 'head'), 0, 0, tiled=True)  33.2 us
    all_to_all x1, blocking collectives, per_device(): far = lax.all_to_all(share, 'block', 0, 0, tiled=True)  23.3 us
    all_to_all x1, starting transfers between devices, swap(): return lax.all_to_all(array, ('near', 'head'), 0, 0, tiled=True)  11.1 us
    pallas_call x1, Pallas kernels, grads_stage(): pl.pallas_call(body, in_specs=[pl.BlockSpec(memory_space=pltpu.SMEM)] + [...  5.34 us
    pallas_call x1, Pallas kernels, local_stage(): pl.pallas_call(body, in_specs=[pl.BlockSpec(memory_space=pltpu.SMEM), pl....  4.86 us
    pallas_call x1, Pallas kernels, spread(): pl.pallas_call(spread_kernel, grid=(heads // GROUP,), in_specs=[wide] * 5...  2.42 us
  transfers between devices with their start and end apart: 1, of which 1 were waited for; matrix products, arithmetic and copies ran while one was open for 0% of the time, Pallas kernels for 0%

profile of v3, /device:TPU:1, one launch (start us, length us, event | category | flops | bytes accessed | tf_op | source)
XLA Modules:
  0.0 119.2 jit_solution(3656526196146519013)
XLA Ops:
  0.6 2.4 %spread.1 = bf16[32,168,128]{2,1,0:T(8,128)(2,1)} custom-call(bf16[32,4096]{1,0:T(8,128)(2,1)} %key_ref.1, bf16[32,4096]{1,0:T(8,128)(2,1)} %decay_ref.1, bf16[32,4096]{1,0:T(8,128)(2,1)} %value_ref.1, bf16[32,4096]{1,0:T(8,128)(2,1)} %query_ref.1, bf16[32,4096]{1,0:T(8,128)(2,1)} %grad_ref.1, bf16[32,32]{1,0:T(8,128)(2,1)} %strength_ref.1), custom_call_target="tpu_custom_call" | custom-call | tf_op jit(solution)/shard_map/spread/pallas_call | solution.py:146
  3.1 11.1 %all-to-all-start = ((bf16[32,168,128]{2,1,0:T(8,128)(2,1)}), bf16[32,168,128]{2,1,0:T(8,128)(2,1)S(1)}, u32[]{:S(2)}, u32[]{:S(2)}) async-start(bf16[32,168,128]{2,1,0:T(8,128)(2,1)} %spread.1), calls=%async_computation | async-start | bytes 2752512 | tf_op jit(solution)/shard_map/all_to_all | solution.py:467
  14.1 33.2 %all-to-all-done.refs_1_ = bf16[32,168,128]{2,1,0:T(8,128)(2,1)S(1)} async-done(((bf16[32,168,128]{2,1,0:T(8,128)(2,1)}), bf16[32,168,128]{2,1,0:T(8,128)(2,1)S(1)}, u32[]{:S(2)}, u32[]{:S(2)}) %all-to-all-start) | async-done | bytes 1376288 | tf_op jit(solution)/shard_map/all_to_all | solution.py:467
  47.3 4.9 %local_stage.1 = (f32[8,256,128]{2,1,0:T(8,128)S(1)}, bf16[4,8,128,256]{3,2,1,0:T(8,128)(2,1)S(1)}, f32[8,128,128]{2,1,0:T(8,128)S(1)}, bf16[14,128,256]{2,1,0:T...) custom-call(s32[1]{0:T(128)} %bitcast.refs_0_, bf16[32,168,128]{2,1,0:T(8,128)(2,1)S(1)} %all-to-all-done.refs_1_), custom_call_target="tpu_custom_call" | custom-call | tf_op jit(solution)/shard_map/local_stage/pallas_call | solution.py:271
  52.2 23.3 %all_to_all.15.refs_2_ = f32[8,256,128]{2,1,0:T(8,128)S(1)} all-to-all(f32[8,256,128]{2,1,0:T(8,128)S(1)} %get-tuple-element.16), channel_id=1, replica_groups=mesh['block'=8,'near'=4,'head'=8] {'block'}, dimensions={0} | all-to-all | bytes 2097152 | tf_op jit(solution)/shard_map/all_to_all | solution.py:471
  75.5 5.3 %grads_stage.1 = bf16[32,136,128]{2,1,0:T(8,128)(2,1)S(1)} custom-call(s32[1]{0:T(128)} %bitcast.refs_0_, bf16[32,168,128]{2,1,0:T(8,128)(2,1)S(1)} %all-to-all-done.refs_1_, f32[8,256,128]{2,1,0:T(8,128)S(1)} %all_to_all.15.refs_2_, bf16[4,8,128,256]{3,2,1,0:T(8,128)(2,1)S(1)} %get-tuple-element.17.refs_3_, f32[8,128,128]{2,1,0:T(8,128)S(1)} %get-tuple-element.18.refs_4_, ...), custom_call_target="tpu_custom_call" | custom-call | tf_op jit(solution)/shard_map/grads_stage/pallas_call | solution.py:418
  80.8 37.4 %all_to_all.16.packed_ref = bf16[32,136,128]{2,1,0:T(8,128)(2,1)S(1)} all-to-all(bf16[32,136,128]{2,1,0:T(8,128)(2,1)S(1)} %grads_stage.1), channel_id=1, replica_groups=mesh['block'=8,'near'=4,'head'=8] {'near','head'}, dimensions={0} | all-to-all | bytes 2228224 | tf_op jit(solution)/shard_map/all_to_all | solution.py:467
  118.2 1.0 unspread.1
Async XLA Ops:
  3.1 44.3 %all-to-all-start = ((bf16[32,168,128]{2,1,0:T(8,128)(2,1)}), bf16[32,168,128]{2,1,0:T(8,128)(2,1)S(1)}, u32[]{:S(2)}, u32[]{:S(2)}) async-start(bf16[32,168,128]{2,1,0:T(8,128)(2,1)} %spread.1), calls=%async_computation | async-start | bytes 2752512 | tf_op jit(solution)/shard_map/all_to_all | solution.py:467

commit v4 on v3

--- a/solution.py
+++ b/solution.py
@@ -302,16 +302,33 @@
     sum_ones = jnp.ones((16, CHUNK), bf16)
     scale = CHUNK ** (-0.5)
     place = place_ref[0]
-    state = jnp.where(place > 0, far_ref[0, CHUNK:], 0.0)
-    cot = jnp.where(place < blocks - 1, far_ref[blocks - 1, CHUNK:], 0.0)
-    for step in range(1, blocks - 1):
-        back = blocks - 1 - step
-        moved = product(parts(far_ref[step, :CHUNK]), parts(state)) + far_ref[step, CHUNK:]
-        returned = product(parts(far_ref[back, :CHUNK]), parts(cot), 0, 0) + far_ref[back, CHUNK:]
-        state = jnp.where(place > step, moved, state)
-        cot = jnp.where(place < back, returned, cot)
-    state_ref[2 * pieces - 2] = state
-    cot_ref[2 * pieces - 2] = cot
+    ready = [None] * pieces
+
+    def relay():
+        state = jnp.where(place > 0, far_ref[0, CHUNK:], 0.0)
+        cot = jnp.where(place < blocks - 1, far_ref[blocks - 1, CHUNK:], 0.0)
+        for step in range(1, blocks - 1):
+            back = blocks - 1 - step
+            moved = product(parts(far_ref[step, :CHUNK]), parts(state)) + far_ref[step, CHUNK:]
+            returned = product(parts(far_ref[back, :CHUNK]), parts(cot), 0, 0) + far_ref[back, CHUNK:]
+            state = jnp.where(place > step, moved, state)
+            cot = jnp.where(place < back, returned, cot)
+            yield
+        state_ref[2 * pieces - 2] = state
+        cot_ref[2 * pieces - 2] = cot
+
+    def prepare(piece):
+        t = key_terms(packed_ref, piece, causal_ones)
+        yield
+        query_one, query_inverse = query_terms(packed_ref, piece)
+        yield
+        fall_parts = parts(t["unit"] * t["fall"])
+        yield
+        from_grad = product(halves(maps_ref[SCORES, piece]), (chunk_of(packed_ref, piece, 4),), 0, 0)
+        yield
+        ready[piece] = (t, query_one, query_inverse, fall_parts, from_grad)
+
+    in_step([relay()] + [prepare(piece) for piece in range(pieces)])
     for parent, left, right in reversed(tree_levels(pieces)):
         state = state_ref[parent]
         cot = cot_ref[parent]
@@ -319,9 +336,9 @@
         state_ref[right] = product(halves(transfer_ref[left]), parts(state)) + left_ref[parent - pieces]
         cot_ref[right] = cot
         cot_ref[left] = product(halves(transfer_ref[right]), parts(cot), 0, 0) + right_ref[parent - pieces]
+
     def work(piece):
-        t = key_terms(packed_ref, piece, causal_ones)
-        query_one, query_inverse = query_terms(packed_ref, piece)
+        t, query_one, query_inverse, fall_parts, from_grad = ready[piece]
         query = query_one * scale
         value = chunk_of(packed_ref, piece, 2).astype(f32)
         grad = chunk_of(packed_ref, piece, 4)
@@ -332,13 +349,12 @@
         cot_parts = parts(cot)
         unit = t["unit"]
         key_rise = unit * t["rise"]
-        key_fall = unit * t["fall"]
         key_head = unit * t["head"]
         key_tail = unit * t["tail"]
         update = wvalue_ref[piece] - product(halves(maps_ref[WKEY, piece]), state_parts)
         yield
         update_parts = parts(update)
-        d_update = product(halves(maps_ref[SCORES, piece]), (grad,), 0, 0) + product(parts(key_tail), cot_parts)
+        d_update = from_grad + product(parts(key_tail), cot_parts)
         yield
         d_right = product(halves(maps_ref[SOLVE, piece]), parts(d_update), 0, 0)
         d_value = t["weight"] * d_right
@@ -356,7 +372,6 @@
         yield
         d_scores_parts = parts(d_scores)
         d_inner_parts = parts(d_inner)
-        fall_parts = parts(key_fall)
         query_rise = query * t["rise"]
         d_query_rise = product(d_scores_parts, fall_parts)
         d_key_rise = product(d_inner_parts, fall_parts)

time: 120 us -> 119 us (level)
  no operation moved by 1% of the time
where the time goes in v4:
time: 119 us
  blocking collectives  60.7 us (51%)
  waiting for transfers between devices  33.2 us (28%)
  Pallas kernels  13.6 us (11%)
  starting transfers between devices  11.1 us (9%)
    all_to_all x1, blocking collectives, swap(): return lax.all_to_all(array, ('near', 'head'), 0, 0, tiled=True)  37.4 us
    all_to_all x1, waiting for transfers between devices, swap(): return lax.all_to_all(array, ('near', 'head'), 0, 0, tiled=True)  33.2 us
    all_to_all x1, blocking collectives, per_device(): far = lax.all_to_all(share, 'block', 0, 0, tiled=True)  23.3 us
    all_to_all x1, starting transfers between devices, swap(): return lax.all_to_all(array, ('near', 'head'), 0, 0, tiled=True)  11.1 us
    pallas_call x1, Pallas kernels, grads_stage(): pl.pallas_call(body, in_specs=[pl.BlockSpec(memory_space=pltpu.SMEM)] + [...  5.3 us
    pallas_call x1, Pallas kernels, local_stage(): pl.pallas_call(body, in_specs=[pl.BlockSpec(memory_space=pltpu.SMEM), pl....  4.86 us
    pallas_call x1, Pallas kernels, spread(): pl.pallas_call(spread_kernel, grid=(heads // GROUP,), in_specs=[wide] * 5...  2.42 us
  transfers between devices with their start and end apart: 1, of which 1 were waited for; matrix products, arithmetic and copies ran while one was open for 0% of the time, Pallas kernels for 0%

profile of v4, /device:TPU:1, one launch (start us, length us, event | category | flops | bytes accessed | tf_op | source)
XLA Modules:
  0.0 119.2 jit_solution(16645027754274925353)
XLA Ops:
  0.6 2.4 %spread.1 = bf16[32,168,128]{2,1,0:T(8,128)(2,1)} custom-call(bf16[32,4096]{1,0:T(8,128)(2,1)} %key_ref.1, bf16[32,4096]{1,0:T(8,128)(2,1)} %decay_ref.1, bf16[32,4096]{1,0:T(8,128)(2,1)} %value_ref.1, bf16[32,4096]{1,0:T(8,128)(2,1)} %query_ref.1, bf16[32,4096]{1,0:T(8,128)(2,1)} %grad_ref.1, bf16[32,32]{1,0:T(8,128)(2,1)} %strength_ref.1), custom_call_target="tpu_custom_call" | custom-call | tf_op jit(solution)/shard_map/spread/pallas_call | solution.py:146
  3.1 11.1 %all-to-all-start = ((bf16[32,168,128]{2,1,0:T(8,128)(2,1)}), bf16[32,168,128]{2,1,0:T(8,128)(2,1)S(1)}, u32[]{:S(2)}, u32[]{:S(2)}) async-start(bf16[32,168,128]{2,1,0:T(8,128)(2,1)} %spread.1), calls=%async_computation | async-start | bytes 2752512 | tf_op jit(solution)/shard_map/all_to_all | solution.py:482
  14.1 33.2 %all-to-all-done.refs_1_ = bf16[32,168,128]{2,1,0:T(8,128)(2,1)S(1)} async-done(((bf16[32,168,128]{2,1,0:T(8,128)(2,1)}), bf16[32,168,128]{2,1,0:T(8,128)(2,1)S(1)}, u32[]{:S(2)}, u32[]{:S(2)}) %all-to-all-start) | async-done | bytes 1376288 | tf_op jit(solution)/shard_map/all_to_all | solution.py:482
  47.3 4.9 %local_stage.1 = (f32[8,256,128]{2,1,0:T(8,128)S(1)}, bf16[4,8,128,256]{3,2,1,0:T(8,128)(2,1)S(1)}, f32[8,128,128]{2,1,0:T(8,128)S(1)}, bf16[14,128,256]{2,1,0:T...) custom-call(s32[1]{0:T(128)} %bitcast.refs_0_, bf16[32,168,128]{2,1,0:T(8,128)(2,1)S(1)} %all-to-all-done.refs_1_), custom_call_target="tpu_custom_call" | custom-call | tf_op jit(solution)/shard_map/local_stage/pallas_call | solution.py:271
  52.2 23.3 %all_to_all.15.refs_2_ = f32[8,256,128]{2,1,0:T(8,128)S(1)} all-to-all(f32[8,256,128]{2,1,0:T(8,128)S(1)} %get-tuple-element.16), channel_id=1, replica_groups=mesh['block'=8,'near'=4,'head'=8] {'block'}, dimensions={0} | all-to-all | bytes 2097152 | tf_op jit(solution)/shard_map/all_to_all | solution.py:486
  75.5 5.3 %grads_stage.1 = bf16[32,136,128]{2,1,0:T(8,128)(2,1)S(1)} custom-call(s32[1]{0:T(128)} %bitcast.refs_0_, bf16[32,168,128]{2,1,0:T(8,128)(2,1)S(1)} %all-to-all-done.refs_1_, f32[8,256,128]{2,1,0:T(8,128)S(1)} %all_to_all.15.refs_2_, bf16[4,8,128,256]{3,2,1,0:T(8,128)(2,1)S(1)} %get-tuple-element.17.refs_3_, f32[8,128,128]{2,1,0:T(8,128)S(1)} %get-tuple-element.18.refs_4_, ...), custom_call_target="tpu_custom_call" | custom-call | tf_op jit(solution)/shard_map/grads_stage/pallas_call | solution.py:433
  80.8 37.4 %all_to_all.16.packed_ref = bf16[32,136,128]{2,1,0:T(8,128)(2,1)S(1)} all-to-all(bf16[32,136,128]{2,1,0:T(8,128)(2,1)S(1)} %grads_stage.1), channel_id=1, replica_groups=mesh['block'=8,'near'=4,'head'=8] {'near','head'}, dimensions={0} | all-to-all | bytes 2228224 | tf_op jit(solution)/shard_map/all_to_all | solution.py:482
  118.2 1.0 unspread.1
Async XLA Ops:
  3.1 44.3 %all-to-all-start = ((bf16[32,168,128]{2,1,0:T(8,128)(2,1)}), bf16[32,168,128]{2,1,0:T(8,128)(2,1)S(1)}, u32[]{:S(2)}, u32[]{:S(2)}) async-start(bf16[32,168,128]{2,1,0:T(8,128)(2,1)} %spread.1), calls=%async_computation | async-start | bytes 2752512 | tf_op jit(solution)/shard_map/all_to_all | solution.py:482
